TPU v7x, 512 devices: a whole 4x8x8 slice. The times are simulated.
512 devices in a mesh: frame: 16 (over x, y_hi, core), patch: 32 (over y_lo, z).
Axes of the slice: x: 4, y: 8 (y_hi: 2, y_lo: 4; y = y_hi * 4 + y_lo), z: 8, core: 2. Of those that a mesh axis runs over, the one named last changes fastest.
Arguments:
- features: bfloat16 [64, 32, 128, 320], P('frame', 'patch'), may hold values from -6 to 6
- stale_edges: bfloat16 [64, 64, 128, 320], P('frame', 'patch'), may hold values from -6 to 6
- conv_weight: bfloat16 [3, 3, 320, 320], P(None, None, None, 'frame'), may hold values from -0.109375 to 0.109375
- conv_bias: float32 [320], replicated, may hold values from -3 to 3
- first_gain: float32 [320], replicated, may hold values from 0.1 to 1.9
- first_shift: float32 [320], replicated, may hold values from -2 to 2
- query_weight: bfloat16 [320, 320], replicated, may hold values from -4 to 4
- key_weight: bfloat16 [320, 320], replicated, may hold values from -4 to 4
- value_weight: bfloat16 [320, 320], replicated, may hold values from -0.3125 to 0.3125
- out_weight: bfloat16 [320, 320], replicated, may hold values from -0.3125 to 0.3125
- out_bias: float32 [320], replicated, may hold values from -2 to 2
- second_gain: float32 [320], replicated, may hold values from 0.1 to 1.9
- second_shift: float32 [320], replicated, may hold values from -2 to 2
- geglu_weight: bfloat16 [320, 2560], replicated, may hold values from -0.3125 to 0.3125
- geglu_bias: float32 [2560], replicated, may hold values from -2 to 2
- down_weight: bfloat16 [1280, 320], replicated, may hold values from -0.15625 to 0.15625
- down_bias: float32 [320], replicated, may hold values from -2 to 2
Outputs:
- block_out: bfloat16 [64, 32, 128, 320], P('frame', 'patch')
All inputs are finite; a program needn't handle non-finite values.
Results may differ from a plain program's by a relative error of at most 0.02.
Values may be sent and summed in bfloat16 or wider, within the bound.
No kernel may reach another device: no remote copies, remote signals or barrier semaphores. Data moves between devices by JAX's collectives and lax.ppermute only.
A program may use at most 64 MiB of HBM per device.

v0:
```python
import math

import jax
import jax.numpy as jnp
from jax import lax
from jax.sharding import PartitionSpec as P

HEADS = 8


def padded_2(shard, sides, width):
    for axis, dim in sides:
        devices, length = (lax.axis_size(axis), shard.shape[dim])
        up = [(i, (i + 1) % devices) for i in range(devices - 1)]
        down = [(j, i) for i, j in up]
        last = lax.slice_in_dim(shard, length - width, length, axis=dim)
        first = lax.slice_in_dim(shard, 0, width, axis=dim)
        before = lax.ppermute(last, axis, up)
        after = lax.ppermute(first, axis, down)
        shard = jnp.concatenate([before, shard, after], axis=dim)
    return shard


def layer_norm(inputs, gain_vec, shift_vec):
    average = jnp.mean(inputs, axis=-1, keepdims=True)
    centred = inputs - average
    variance = jnp.mean(centred * centred, axis=-1, keepdims=True)
    return centred * lax.rsqrt(variance + 1e-05) * gain_vec + shift_vec


def position_table(positions, channels):
    halves = jnp.arange(channels // 2).astype(jnp.float32)
    rates = jnp.exp(halves * (-2.0 * math.log(10000.0) / channels))
    angles = positions[:, None] * rates[None, :]
    return jnp.stack([jnp.sin(angles), jnp.cos(angles)], axis=-1).reshape(
        positions.shape[0], channels
    )


def project(block, weight):
    flat = block.reshape(-1, block.shape[-1])
    return (
        jnp.dot(flat, weight, preferred_element_type=jnp.float32)
        .astype(jnp.bfloat16)
        .reshape(block.shape)
    )


def attend(queries, key_rows, value_rows):
    frame_count, pixel_count, channels = queries.shape
    head_dim = channels // HEADS
    shaped = (frame_count, pixel_count, HEADS, head_dim)
    scores = jnp.einsum(
        "fnhd,gnhd->nhfg",
        queries.reshape(shaped),
        key_rows.reshape(shaped),
        preferred_element_type=jnp.float32,
    ) / math.sqrt(head_dim)
    scores = scores - jnp.max(scores, axis=-1, keepdims=True)
    expo_scores = jnp.exp(scores)
    attn_probs = (expo_scores / jnp.sum(expo_scores, axis=-1, keepdims=True)).astype(jnp.bfloat16)
    context = jnp.einsum(
        "nhfg,gnhd->fnhd",
        attn_probs,
        value_rows.reshape(shaped),
        preferred_element_type=jnp.float32,
    )
    return context.astype(jnp.bfloat16).reshape(frame_count, pixel_count, channels)


def per_device(
    features,
    stale_edges,
    conv_weight,
    conv_bias,
    first_gain,
    first_shift,
    query_weight,
    key_weight,
    value_weight,
    out_weight,
    out_bias,
    second_gain,
    second_shift,
    geglu_weight,
    geglu_bias,
    down_weight,
    down_bias,
):
    frame_count, band_rows, columns, channels = features.shape
    rim_rows = padded_2(stale_edges, (("patch", 1),), 1)
    padded = jnp.concatenate([rim_rows[:, 0:1], features, rim_rows[:, 3:4]], axis=1)
    padded = jnp.pad(padded, ((0, 0), (0, 0), (1, 1), (0, 0)))
    windows = []
    for row_step in range(3):
        for col_step in range(3):
            windows.append(
                padded[:, row_step : row_step + band_rows, col_step : col_step + columns].reshape(
                    -1, channels
                )
            )
    full_kernel = lax.all_gather(conv_weight, "frame", axis=3, tiled=True)
    summed = jnp.zeros((windows[0].shape[0], full_kernel.shape[3]), jnp.float32)
    for row_step in range(3):
        for col_step in range(3):
            summed = summed + jnp.dot(
                windows[3 * row_step + col_step],
                full_kernel[row_step, col_step],
                preferred_element_type=jnp.float32,
            )
    conv_out = (summed + conv_bias).astype(jnp.bfloat16)
    pixel_count = band_rows * columns
    groups = lax.axis_size("frame")
    tokens = conv_out.reshape(frame_count, pixel_count, channels)
    positions = (lax.axis_index("frame") * frame_count + jnp.arange(frame_count)).astype(
        jnp.float32
    )
    normed = (
        layer_norm(tokens.astype(jnp.float32), first_gain, first_shift)
        + position_table(positions, channels)[:, None, :]
    )
    normed = normed.astype(jnp.bfloat16)
    grouped_shape = (frame_count, groups, pixel_count // groups, channels)
    queries = project(normed, query_weight).reshape(grouped_shape)
    key_rows = project(normed, key_weight).reshape(grouped_shape)
    value_rows = project(normed, value_weight).reshape(grouped_shape)
    outgoing = attend(
        lax.all_to_all(queries, "frame", split_axis=1, concat_axis=0, tiled=True)[:, 0],
        lax.all_to_all(key_rows, "frame", split_axis=1, concat_axis=0, tiled=True)[:, 0],
        lax.all_to_all(value_rows, "frame", split_axis=1, concat_axis=0, tiled=True)[:, 0],
    )[:, None]
    returned = lax.all_to_all(outgoing, "frame", split_axis=0, concat_axis=1, tiled=True).reshape(
        -1, channels
    )
    attn_out = (
        jnp.dot(returned, out_weight, preferred_element_type=jnp.float32) + out_bias
    ).astype(jnp.bfloat16)
    middle = (
        tokens.reshape(-1, channels).astype(jnp.float32) + attn_out.astype(jnp.float32)
    ).astype(jnp.bfloat16)
    normed_two = layer_norm(middle.astype(jnp.float32), second_gain, second_shift).astype(
        jnp.bfloat16
    )
    projected = jnp.dot(normed_two, geglu_weight, preferred_element_type=jnp.float32) + geglu_bias
    inner = geglu_weight.shape[1] // 2
    hidden = (projected[:, :inner] * jax.nn.gelu(projected[:, inner:], approximate=False)).astype(
        jnp.bfloat16
    )
    output = (
        middle.astype(jnp.float32)
        + jnp.dot(hidden, down_weight, preferred_element_type=jnp.float32)
        + down_bias
    )
    return output.astype(jnp.bfloat16).reshape(frame_count, band_rows, columns, channels)


def solution(mesh):
    return jax.shard_map(
        per_device,
        mesh=mesh,
        in_specs=(
            P("frame", "patch", None, None),
            P("frame", "patch", None, None),
            P(None, None, None, "frame"),
            P(),
            P(),
            P(),
            P(),
            P(),
            P(),
            P(),
            P(),
            P(),
            P(),
            P(),
            P(),
            P(),
            P(),
        ),
        out_specs=P("frame", "patch", None, None),
        check_vma=False,
    )
```

profile of v0, /device:TPU:17, one launch (start us, length us, event | category | flops | bytes accessed | tf_op | source)
XLA Modules:
  0.0 220.0 jit_solution(12407874669576983417)
XLA Ops:
  10.2 4.0 %collective-permute-start = (bf16[4,1,128,320]{2,3,1,0:T(8,128)(2,1)}, bf16[4,1,128,320]{2,3,1,0:T(8,128)(2,1)S(1)}, u32[]{:S(2)}, u32[]{:S(2)}) collective-permute-start(bf16[4,1,128,320]{2,3,1,0:T(8,128)(2,1)} %get-tuple-element.20), channel_id=1, source_target_pairs={{0,1},{1,2},{2,3},{3,4},{4,5},{5,6},{6,7},{7,8},{8,9},{9,10},{10,1... | collective-permute-start | bytes 983048 | tf_op jit(solution)/shard_map/ppermute | solution.py:18
  14.2 8.5 %collective-permute-start.1 = (bf16[4,1,128,320]{2,3,1,0:T(8,128)(2,1)S(1)}, bf16[4,1,128,320]{2,3,1,0:T(8,128)(2,1)S(1)}, u32[]{:S(2)}, u32[]{:S(2)}) collective-permute-start(bf16[4,1,128,320]{2,3,1,0:T(8,128)(2,1)S(1)} %get-tuple-element.21), channel_id=1, source_target_pairs={{1,0},{2,1},{3,2},{4,3},{5,4},{6,5},{7,6},{8,7},{9,8},{10,9},{11,1... | collective-permute-start | bytes 983048 | tf_op jit(solution)/shard_map/ppermute | solution.py:19
  24.9 3.5 %collective-permute-done = bf16[4,1,128,320]{2,3,1,0:T(8,128)(2,1)S(1)} collective-permute-done((bf16[4,1,128,320]{2,3,1,0:T(8,128)(2,1)}, bf16[4,1,128,320]{2,3,1,0:T(8,128)(2,1)S(1)}, u32[]{:S(2)}, u32[]{:S(2)}) %collective-permute-start) | collective-permute-done | bytes 327712 | tf_op jit(solution)/shard_map/ppermute | solution.py:18
  38.5 49.3 %all-gather.2.cloned.1.call-done = bf16[3,3,320,320]{2,1,0,3:T(4,128)(2,1)} async-done(((bf16[3,3,320,20]{2,1,0,3:T(4,128)(2,1)}), bf16[3,3,320,320]{2,1,0,3:T(4,128)(2,1)}) %all-gather.2.cloned.1.call-update) | async-done | bytes 1843216 | tf_op jit(solution)/shard_map/all_gather | solution.py:102
  87.8 8.0 %fusion.122 = (bf16[1,1,320,320]{2,1,0,3:T(2,128)(2,1)S(1)}, bf16[1,1,320,320]{2,1,0,3:T(2,128)(2,1)S(1)}, bf16[1,1,320,320]{2,1,0,3:T(2,128)(2,1)S(1)}, bf16[1,...) fusion(bf16[3,3,320,320]{2,1,0,3:T(4,128)(2,1)} %all-gather.2.c, ...), kind=kLoop, calls=%fused_computation.143 | loop fusion | bytes 3686400 | tf_op jit(solution)/shard_map/slice | solution.py:108
  95.7 2.0 copy.102
  99.6 2.0 copy.104
  101.6 1.9 copy.105
  119.1 5.8 %all-to-all-start.1 = ((bf16[4,16,8,320]{3,2,0,1:T(8,128)(2,1)}), bf16[4,16,8,320]{3,2,0,1:T(8,128)(2,1)S(1)}, u32[]{:S(2)}, u32[]{:S(2)}) async-start(bf16[4,16,8,320]{3,2,0,1:T(8,128)(2,1)} %copy.91), calls=%async_computation.1 | async-start | bytes 786432 | tf_op jit(solution)/shard_map/all_to_all | solution.py:128
  124.9 2.0 convolution_convert_fusion.1
  128.9 11.9 %all-to-all-done.1 = bf16[4,16,8,320]{3,2,0,1:T(8,128)(2,1)S(1)} async-done(((bf16[4,16,8,320]{3,2,0,1:T(8,128)(2,1)}), bf16[4,16,8,320]{3,2,0,1:T(8,128)(2,1)S(1)}, u32[]{:S(2)}, u32[]{:S(2)}) %all-to-all-start.1) | async-done | bytes 327712 | tf_op jit(solution)/shard_map/all_to_all | solution.py:128
  140.8 4.4 %all-to-all-start.2 = ((bf16[4,16,8,320]{3,2,0,1:T(8,128)(2,1)}), bf16[4,16,8,320]{3,2,0,1:T(8,128)(2,1)}, u32[]{:S(2)}, u32[]{:S(2)}) async-start(bf16[4,16,8,320]{3,2,0,1:T(8,128)(2,1)} %copy.93), calls=%async_computation.2 | async-start | bytes 786432 | tf_op jit(solution)/shard_map/all_to_all | solution.py:129
  145.1 2.0 convolution_convert_fusion.3
  149.2 2.0 reshape_squeeze.10
  151.2 8.0 %all-to-all-done.2 = bf16[4,16,8,320]{3,2,0,1:T(8,128)(2,1)} async-done(((bf16[4,16,8,320]{3,2,0,1:T(8,128)(2,1)}), bf16[4,16,8,320]{3,2,0,1:T(8,128)(2,1)}, u32[]{:S(2)}, u32[]{:S(2)}) %all-to-all-start.2) | async-done | bytes 327712 | tf_op jit(solution)/shard_map/all_to_all | solution.py:129
  159.2 4.4 %all-to-all-start = ((bf16[4,16,8,320]{3,2,0,1:T(8,128)(2,1)}), bf16[4,16,8,320]{3,2,0,1:T(8,128)(2,1)}, u32[]{:S(2)}, u32[]{:S(2)}) async-start(bf16[4,16,8,320]{3,2,0,1:T(8,128)(2,1)} %copy.89), calls=%async_computation | async-start | bytes 786432 | tf_op jit(solution)/shard_map/all_to_all | solution.py:130
  163.6 2.7 %reshape_squeeze.11 = bf16[64,8,8,40]{3,2,1,0:T(8,128)(2,1)} reshape(bf16[16,4,1,8,320]{4,3,1,0,2:T(8,128)(2,1)} %bitcast.18) | data formatting | bytes 655360 | tf_op jit(solution)/shard_map/reshape;squeeze | solution.py:56
  166.3 3.2 %fusion.126 = f32[8,8,64]{2,1,0:T(8,128)S(1)} fusion(bf16[64,8,8,40]{3,2,1,0:T(8,128)(2,1)} %reshape_squeeze.11, bf16[64,8,8,40]{3,2,1,0:T(8,128)(2,1)S(1)} %reshape_squeeze.10), kind=kOutput, calls=%fused_computation.147 | convolution fusion | flops 21758016 | bytes 671744 | tf_op jit(solution)/shard_map/sub | solution.py:59
  169.5 3.9 %fusion.39 = f32[8,8,64,64]{2,3,1,0:T(8,128)} fusion(bf16[64,8,8,40]{3,2,1,0:T(8,128)(2,1)} %reshape_squeeze.11, bf16[64,8,8,40]{3,2,1,0:T(8,128)(2,1)S(1)} %reshape_squeeze.10), kind=kOutput, calls=%fused_computation.60 | convolution fusion | flops 20971520 | bytes 1703936 | tf_op jit(solution)/shard_map/fnhd,gnhd->nhfg/dot_general | solution.py:53
  173.4 4.3 %all-to-all-done = bf16[4,16,8,320]{3,2,0,1:T(8,128)(2,1)} async-done(((bf16[4,16,8,320]{3,2,0,1:T(8,128)(2,1)}), bf16[4,16,8,320]{3,2,0,1:T(8,128)(2,1)}, u32[]{:S(2)}, u32[]{:S(2)}) %all-to-all-start) | async-done | bytes 327712 | tf_op jit(solution)/shard_map/all_to_all | solution.py:130
  177.7 2.0 reshape_squeeze.9
  179.6 3.7 %convolution_convert_fusion = bf16[8,8,40,64]{3,2,1,0:T(8,128)(2,1)} fusion(bf16[64,8,8,40]{3,2,1,0:T(8,128)(2,1)S(1)} %reshape_squeeze.9, f32[8,8,64]{2,1,0:T(8,128)S(1)} %fusion.126, f32[8,8,64,64]{2,3,1,0:T(8,128)} %fusion.39), kind=kOutput, calls=%fused_computation.34 | convolution fusion | flops 22188096 | bytes 1720320 | tf_op jit(solution)/shard_map/nhfg,gnhd->fnhd/dot_general | solution.py:62
  184.9 19.1 %all_to_all.60 = bf16[64,1,8,320]{3,2,1,0:T(8,128)(2,1)S(1)} all-to-all(bf16[64,1,8,320]{3,2,1,0:T(8,128)(2,1)S(1)} %copy.98), channel_id=1, replica_groups=mesh['frame'=16,'patch'=32] {'frame'}, dimensions={0} | all-to-all | bytes 655360 | tf_op jit(solution)/shard_map/all_to_all | solution.py:132
  206.3 5.9 %fusion.35 = bf16[512,320]{0,1:T(8,128)(2,1)S(1)} fusion(f32[512,320]{0,1:T(8,128)S(1)} %get-tuple-element.27, bf16[1280,320]{0,1:T(8,128)(2,1)S(1)} %copy-done.22, f32[512,2560]{1,0:T(8,128)S(1)} %convolution_add_fusion, f32[320]{0:T(512)S(1)} %copy-done.26), kind=kOutput, calls=%fused_computation.58 | convolution fusion | flops 463175680 | bytes 7046400 | tf_op jit(solution)/shard_map/dot_general | solution.py:151
  (111 shorter events, 41.6 us)
Async XLA Ops:
  6.5 198.0 %copy-start = (bf16[320,2560]{1,0:T(8,128)(2,1)S(1)}, bf16[320,2560]{1,0:T(8,128)(2,1)}, u32[]{:S(2)}) copy-start(bf16[320,2560]{1,0:T(8,128)(2,1)} %param.30) | copy-start | bytes 4915204
  6.5 22.5 %copy-start.8 = (bf16[4,1,128,320]{2,3,1,0:T(8,128)(2,1)S(1)}, bf16[4,1,128,320]{2,3,1,0:T(8,128)(2,1)}, u32[]{:S(2)}) copy-start(bf16[4,1,128,320]{2,3,1,0:T(8,128)(2,1)} %param.17) | copy-start | bytes 983044
  6.5 81.2 %all-gather.2.cloned.1.call-start = ((), (), s32[]{:S(2)}) async-start(), calls=%async_computation.4 | async-start | bytes 3133440 | tf_op jit(solution)/shard_map/all_gather | solution.py:102
  10.2 18.2 %collective-permute-start = (bf16[4,1,128,320]{2,3,1,0:T(8,128)(2,1)}, bf16[4,1,128,320]{2,3,1,0:T(8,128)(2,1)S(1)}, u32[]{:S(2)}, u32[]{:S(2)}) collective-permute-start(bf16[4,1,128,320]{2,3,1,0:T(8,128)(2,1)} %get-tuple-element.20), channel_id=1, source_target_pairs={{0,1},{1,2},{2,3},{3,4},{4,5},{5,6},{6,7},{7,8},{8,9},{9,10},{10,1... | collective-permute-start | bytes 983048 | tf_op jit(solution)/shard_map/ppermute | solution.py:18
  14.2 14.8 %collective-permute-start.1 = (bf16[4,1,128,320]{2,3,1,0:T(8,128)(2,1)S(1)}, bf16[4,1,128,320]{2,3,1,0:T(8,128)(2,1)S(1)}, u32[]{:S(2)}, u32[]{:S(2)}) collective-permute-start(bf16[4,1,128,320]{2,3,1,0:T(8,128)(2,1)S(1)} %get-tuple-element.21), channel_id=1, source_target_pairs={{1,0},{2,1},{3,2},{4,3},{5,4},{6,5},{7,6},{8,7},{9,8},{10,9},{11,1... | collective-permute-start | bytes 983048 | tf_op jit(solution)/shard_map/ppermute | solution.py:19
  108.8 5.2 %copy-start.7 = (bf16[4,1,128,320]{2,0,3,1:T(4,128)(2,1)S(1)}, bf16[4,1,128,320]{2,0,3,1:T(4,128)(2,1)}, u32[]{:S(2)}) copy-start(bf16[4,1,128,320]{2,0,3,1:T(4,128)(2,1)} %copy.73) | copy-start | bytes 983044
  111.0 3.0 %copy-start.14 = (bf16[1,1,320,320]{3,2,1,0:T(8,128)(2,1)S(1)}, bf16[1,1,320,320]{3,2,1,0:T(8,128)(2,1)}, u32[]{:S(2)}) copy-start(bf16[1,1,320,320]{3,2,1,0:T(8,128)(2,1)} %copy.104) | copy-start | bytes 614404
  111.0 3.4 %copy-start.6 = (bf16[4,1,128,320]{2,0,3,1:T(4,128)(2,1)S(1)}, bf16[4,1,128,320]{2,0,3,1:T(4,128)(2,1)}, u32[]{:S(2)}) copy-start(bf16[4,1,128,320]{2,0,3,1:T(4,128)(2,1)} %copy.75) | copy-start | bytes 983044
  111.0 3.4 %copy-start.13 = (bf16[1,1,320,320]{3,2,1,0:T(8,128)(2,1)S(1)}, bf16[1,1,320,320]{3,2,1,0:T(8,128)(2,1)}, u32[]{:S(2)}) copy-start(bf16[1,1,320,320]{3,2,1,0:T(8,128)(2,1)} %copy.105) | copy-start | bytes 614404
  112.5 2.3 %copy-start.12 = (bf16[1,1,320,320]{3,2,1,0:T(8,128)(2,1)S(1)}, bf16[1,1,320,320]{3,2,1,0:T(8,128)(2,1)}, u32[]{:S(2)}) copy-start(bf16[1,1,320,320]{3,2,1,0:T(8,128)(2,1)} %copy.106) | copy-start | bytes 614404
  115.3 1.3 copy-start.2
  116.2 1.4 copy-start.19
  116.2 1.4 copy-start.20
  119.1 21.6 %all-to-all-start.1 = ((bf16[4,16,8,320]{3,2,0,1:T(8,128)(2,1)}), bf16[4,16,8,320]{3,2,0,1:T(8,128)(2,1)S(1)}, u32[]{:S(2)}, u32[]{:S(2)}) async-start(bf16[4,16,8,320]{3,2,0,1:T(8,128)(2,1)} %copy.91), calls=%async_computation.1 | async-start | bytes 786432 | tf_op jit(solution)/shard_map/all_to_all | solution.py:128
  140.8 8.4 %copy-start.1 = (bf16[4,16,8,320]{3,2,0,1:T(8,128)(2,1)}, bf16[4,16,8,320]{3,2,0,1:T(8,128)(2,1)S(1)}, u32[]{:S(2)}) copy-start(bf16[4,16,8,320]{3,2,0,1:T(8,128)(2,1)S(1)} %all-to-all-done.1) | copy-start | bytes 983044
  140.8 18.4 %all-to-all-start.2 = ((bf16[4,16,8,320]{3,2,0,1:T(8,128)(2,1)}), bf16[4,16,8,320]{3,2,0,1:T(8,128)(2,1)}, u32[]{:S(2)}, u32[]{:S(2)}) async-start(bf16[4,16,8,320]{3,2,0,1:T(8,128)(2,1)} %copy.93), calls=%async_computation.2 | async-start | bytes 786432 | tf_op jit(solution)/shard_map/all_to_all | solution.py:129
  159.2 18.5 %all-to-all-start = ((bf16[4,16,8,320]{3,2,0,1:T(8,128)(2,1)}), bf16[4,16,8,320]{3,2,0,1:T(8,128)(2,1)}, u32[]{:S(2)}, u32[]{:S(2)}) async-start(bf16[4,16,8,320]{3,2,0,1:T(8,128)(2,1)} %copy.89), calls=%async_computation | async-start | bytes 786432 | tf_op jit(solution)/shard_map/all_to_all | solution.py:130
  183.4 20.7 %copy-start.17 = (bf16[320,320]{1,0:T(8,128)(2,1)S(1)}, bf16[320,320]{1,0:T(8,128)(2,1)}, u32[]{:S(2)}) copy-start(bf16[320,320]{1,0:T(8,128)(2,1)} %param.26) | copy-start | bytes 614404
  183.4 20.7 %copy-start.21 = (f32[320]{0:T(512)S(1)}, f32[320]{0:T(512)}, u32[]{:S(2)}) copy-start(f32[320]{0:T(512)} %param.27) | copy-start | bytes 3844
  183.4 21.2 %copy-start.23 = (f32[2560]{0:T(1024)S(1)}, f32[2560]{0:T(1024)}, u32[]{:S(2)}) copy-start(f32[2560]{0:T(1024)} %param.31) | copy-start | bytes 30724
  183.4 21.2 %copy-start.24 = (f32[320]{0:T(512)S(1)}, f32[320]{0:T(512)}, u32[]{:S(2)}) copy-start(f32[320]{0:T(512)} %param.29) | copy-start | bytes 3844
  183.4 21.2 %copy-start.25 = (f32[320]{0:T(512)S(1)}, f32[320]{0:T(512)}, u32[]{:S(2)}) copy-start(f32[320]{0:T(512)} %param.28) | copy-start | bytes 3844
  204.6 1.7 copy-start.22
  204.6 1.7 copy-start.26
  (9 other events, 11.1 us)
Sparse Core Ops, SparseCore 0:
  10.6 77.1 all-gather.1
where the time goes:
time: 221 us; the launch traced here: 220 us
  waiting for transfers between devices  77.6 us (35%)
  local copies, waits for them, and re-layouts  51.8 us (23%)
  matrix products  29 us (13%)
  starting transfers between devices  27 us (12%)
  blocking collectives  19.1 us (9%)
  between operations  14 us (6%)
    all_gather x1, waiting for transfers between devices, per_device(): full_kernel = lax.all_gather(conv_weight, 'frame', axis=3, tiled=True)  49.3 us
    all_to_all x1, blocking collectives, per_device(): lax.all_to_all(outgoing, 'frame', split_axis=0, concat_axis=1, tiled=True)  19.1 us
    unnamed x65, local copies, waits for them, and re-layouts  18.4 us
    all_to_all x1, waiting for transfers between devices, per_device(): lax.all_to_all(queries, 'frame', split_axis=1, concat_axis=0, tiled=True)  11.9 us
    ppermute x1, starting transfers between devices, padded_2(): after = lax.ppermute(first, axis, down)  8.47 us
    all_to_all x1, waiting for transfers between devices, per_device(): lax.all_to_all(key_rows, 'frame', split_axis=1, concat_axis=0, tiled=True)  8.04 us
    slice x1, local copies, waits for them, and re-layouts, per_device(): full_kernel[row_step, col_step]  7.95 us
    slice x7, local copies, waits for them, and re-layouts, per_device(): padded[:, row_step:row_step + band_rows, col_step:col_step + columns]  6.41 us
  transfers between devices with their start and end apart: 6, of which 6 were waited for; matrix products, arithmetic and copies ran while one was open for 15% of the time, Pallas kernels for 0%

commit v1 on v0

v1 whole, which is shorter than its diff:
```python
import functools
import math

import jax
import jax.numpy as jnp
import numpy as np
from jax import lax
from jax.experimental import pallas as pl
from jax.experimental.pallas import tpu as pltpu
from jax.sharding import Mesh, PartitionSpec as P

HEADS = 8
CH = 320
FF = 1280
TAPS_IN = 960
TAPS_PAD = 1024
SLOT = 24
SHARE = 20
FRAMES = 64
COLS = 128
PATCHES = 32
MIB = 1024 * 1024


def pack_weight_kernel(w_ref, out_ref):
    for b in range(3):
        rows = jnp.concatenate(
            [w_ref[a, b].astype(jnp.float32) for a in range(3)]
            + [jnp.zeros((SHARE, TAPS_PAD - TAPS_IN), jnp.float32)],
            axis=1,
        )
        rows = jnp.concatenate(
            [rows, jnp.zeros((SLOT - SHARE, TAPS_PAD), jnp.float32)], axis=0
        )
        out_ref[:, b * TAPS_PAD : (b + 1) * TAPS_PAD] = rows.astype(jnp.bfloat16)


def tokens_kernel(above_ref, band_ref, below_ref, out_ref):
    for f in range(4):
        stacked = jnp.concatenate(
            [above_ref[f], band_ref[f], below_ref[f], jnp.zeros((TAPS_PAD - TAPS_IN, COLS), jnp.bfloat16)],
            axis=0,
        )
        out_ref[f * COLS : (f + 1) * COLS, :] = stacked.T


def conv_kernel(x_ref, sibling_ref, w_ref, bias_ref, sel_ref, out_ref):
    x = jnp.concatenate([x_ref[...], sibling_ref[...]], axis=0)
    tokens = x.shape[0]
    position = lax.broadcasted_iota(jnp.int32, (tokens, 1), 0) % COLS

    def taps(b):
        weight = w_ref[:, :, b * TAPS_PAD : (b + 1) * TAPS_PAD].reshape(-1, TAPS_PAD)
        return lax.dot_general(
            x, weight, (((1,), (1,)), ((), ())), preferred_element_type=jnp.float32
        )

    left = jnp.where(position == 0, 0.0, pltpu.roll(taps(0), 1, 0))
    right = jnp.where(position == COLS - 1, 0.0, pltpu.roll(taps(2), tokens - 1, 0))
    summed = taps(1) + left + right + bias_ref[...]
    ordered = jnp.dot(
        summed.astype(jnp.bfloat16), sel_ref[...], preferred_element_type=jnp.float32
    )
    by_owner = ordered.reshape(2, 2, 2, 16, 8, CH // 2)
    for k in range(16):
        groups = [
            jnp.concatenate([by_owner[core, high, 0, k], by_owner[core, high, 1, k]], axis=0)
            for core in range(2)
            for high in range(2)
        ]
        out_ref[k] = jnp.concatenate(groups, axis=1).astype(jnp.bfloat16)


def norm_rows(values, gain, shift):
    average = jnp.mean(values, axis=-1, keepdims=True)
    centred = values - average
    variance = jnp.mean(centred * centred, axis=-1, keepdims=True)
    return centred * lax.rsqrt(variance + 1e-05) * gain + shift


def block_kernel(
    x_ref,
    order_ref,
    position_ref,
    first_gain_ref,
    first_shift_ref,
    query_ref,
    key_ref,
    value_ref,
    out_weight_ref,
    out_bias_ref,
    second_gain_ref,
    second_shift_ref,
    geglu_ref,
    geglu_bias_ref,
    down_ref,
    down_bias_ref,
    out_ref,
    rows_ref,
    context_ref,
):
    pixels = 8
    blocks = 2 * CH // 128
    half = CH // 2
    received = x_ref[...].astype(jnp.float32).reshape(8, 2, 16, 2 * CH)
    for core in range(2):
        for i in range(blocks):
            rows_ref[core, i] = received[:, core, :, i * 128 : (i + 1) * 128].reshape(128, 128)
    x = jnp.zeros((pixels * FRAMES, CH), jnp.float32)
    for core in range(2):
        pieces = []
        for p in range(pixels):
            row = jnp.concatenate(
                [rows_ref[core, i, pl.ds(p, 16, stride=pixels), :] for i in range(blocks)], axis=1
            )
            for owner_core in range(2):
                for high in range(2):
                    group = (owner_core ^ core) * 2 + high
                    pieces.append(row[:, group * half : (group + 1) * half])
        x += jnp.dot(
            jnp.concatenate(pieces, axis=0).astype(jnp.bfloat16),
            order_ref[core],
            preferred_element_type=jnp.float32,
        )
    position = position_ref[...]
    normed = norm_rows(x, first_gain_ref[...], first_shift_ref[...]).reshape(pixels, FRAMES, CH)
    normed = (normed + position[None]).reshape(pixels * FRAMES, CH).astype(jnp.bfloat16)

    def project(weight_ref):
        return jnp.dot(normed, weight_ref[...], preferred_element_type=jnp.float32).astype(
            jnp.bfloat16
        )

    queries, key_rows, value_rows = project(query_ref), project(key_ref), project(value_ref)
    head_dim = CH // HEADS
    channel = lax.broadcasted_iota(jnp.int32, (1, CH), 1)
    head_masks = [
        (channel >= h * head_dim) & (channel < (h + 1) * head_dim) for h in range(HEADS)
    ]
    for p in range(pixels):
        rows = slice(p * FRAMES, (p + 1) * FRAMES)
        query = queries[rows]
        stacked = jnp.concatenate(
            [jnp.where(m, query, jnp.zeros_like(query)) for m in head_masks], axis=0
        )
        scores = lax.dot_general(
            stacked, key_rows[rows], (((1,), (1,)), ((), ())), preferred_element_type=jnp.float32
        ) * (1.0 / math.sqrt(head_dim))
        expo = jnp.exp(scores - jnp.max(scores, axis=-1, keepdims=True))
        probs = (expo / jnp.sum(expo, axis=-1, keepdims=True)).astype(jnp.bfloat16)
        mixed = jnp.dot(probs, value_rows[rows], preferred_element_type=jnp.float32)
        context = jnp.zeros((FRAMES, CH), jnp.float32)
        for h in range(HEADS):
            context = jnp.where(head_masks[h], mixed[h * FRAMES : (h + 1) * FRAMES], context)
        context_ref[rows, :] = context.astype(jnp.bfloat16)
    attn_out = (
        jnp.dot(context_ref[...], out_weight_ref[...], preferred_element_type=jnp.float32)
        + out_bias_ref[...]
    ).astype(jnp.bfloat16)
    middle = (x + attn_out.astype(jnp.float32)).astype(jnp.bfloat16).astype(jnp.float32)
    normed_two = norm_rows(middle, second_gain_ref[...], second_shift_ref[...]).astype(jnp.bfloat16)
    total = middle + down_bias_ref[...]
    step = 256
    for start in range(0, FF, step):
        lanes = slice(start, start + step)
        gates = slice(FF + start, FF + start + step)
        value = (
            jnp.dot(normed_two, geglu_ref[:, lanes], preferred_element_type=jnp.float32)
            + geglu_bias_ref[:, lanes]
        )
        gate = (
            jnp.dot(normed_two, geglu_ref[:, gates], preferred_element_type=jnp.float32)
            + geglu_bias_ref[:, gates]
        )
        hidden = value * (0.5 * gate * (1.0 + lax.erf(gate * (1.0 / math.sqrt(2.0)))))
        total = total + jnp.dot(
            hidden.astype(jnp.bfloat16), down_ref[lanes, :], preferred_element_type=jnp.float32
        )
    for core in range(2):
        for p in range(pixels):
            start = p * FRAMES + core * 32
            both = jnp.concatenate([total[start : start + 16], total[start + 16 : start + 32]], axis=1)
            for i in range(blocks):
                rows_ref[core, i, pl.ds(p, 16, stride=pixels), :] = both[:, i * 128 : (i + 1) * 128]
        for i in range(blocks):
            out_ref[:, core, :, i * 128 : (i + 1) * 128] = (
                rows_ref[core, i].astype(jnp.bfloat16).reshape(8, 16, 128)
            )


def finish_kernel(x_ref, out_ref):
    received = x_ref[...].astype(jnp.float32)
    for half in range(2):
        lanes = slice(half * CH, (half + 1) * CH)
        for f in range(2):
            rows = received[:, f * 8 : (f + 1) * 8, lanes].reshape(COLS, CH)
            out_ref[half * 2 + f] = rows.T.astype(jnp.bfloat16)


def call(kernel, out_shape, flops, scratch=(), dtype=jnp.bfloat16):
    return pl.pallas_call(
        kernel,
        out_shape=jax.ShapeDtypeStruct(out_shape, dtype),
        scratch_shapes=list(scratch),
        compiler_params=pltpu.CompilerParams(vmem_limit_bytes=48 * MIB),
        cost_estimate=pl.CostEstimate(flops=flops, bytes_accessed=4 * MIB, transcendentals=0),
    )


def position_rows():
    frames = np.array(
        [
            (chip * 2 + core) * 4 + high * 2 + low
            for core in range(2)
            for high in range(2)
            for chip in range(8)
            for low in range(2)
        ]
    )
    rates = 10000.0 ** (-2.0 * np.arange(CH // 2) / CH)
    angles = frames[:, None] * rates[None, :]
    return np.stack([np.sin(angles), np.cos(angles)], axis=-1).reshape(FRAMES, CH).astype(np.float32)


def channel_order():
    order = np.zeros((2, CH // 2, CH), np.float32)
    for core in range(2):
        for chip in range(8):
            for o in range(SHARE):
                order[core, chip * SHARE + o, (chip * 2 + core) * SHARE + o] = 1.0
    return order


def per_device(
    features,
    stale_edges,
    conv_weight,
    conv_bias,
    first_gain,
    first_shift,
    query_weight,
    key_weight,
    value_weight,
    out_weight,
    out_bias,
    second_gain,
    second_shift,
    geglu_weight,
    geglu_bias,
    down_weight,
    down_bias,
):
    frame = ("x", "yh", "c")
    patch = ("yl", "z")
    packed = call(pack_weight_kernel, (SLOT, 3 * TAPS_PAD), 10**6)(
        conv_weight.transpose(0, 1, 3, 2)
    )
    mirrored = [(h * 4 + l, (1 - h) * 4 + 3 - l) for h in range(2) for l in range(4)]
    other = lax.ppermute(packed, ("yh", "yl"), mirrored)
    pair = jnp.stack([packed, other])
    ring = [pair] + [
        lax.ppermute(pair, "x", [((x + j) % 4, x) for x in range(4)]) for j in (1, 2, 3)
    ]
    weight = jnp.concatenate(ring)
    x, yh, c = (lax.axis_index(a) for a in frame)
    chips = jnp.stack([((x + jx) % 4) * 2 + (yh ^ jy) for jx in range(4) for jy in range(2)])
    lane = jnp.arange(SLOT)[None, :]
    target = jnp.where(lane < SHARE, chips[:, None] * SHARE + lane, -1).reshape(-1, 1)
    chosen = target == jnp.arange(CH // 2)[None, :]
    sel = chosen.astype(jnp.bfloat16)
    core_bias = jnp.where(c == 0, *(conv_bias.reshape(8, 2, SHARE)[:, i].reshape(1, -1) for i in range(2)))
    slot_bias = jnp.sum(jnp.where(chosen, core_bias, 0.0), axis=1)[None, :]

    above = lax.ppermute(
        stale_edges[:, 1].transpose(0, 2, 1), patch, [(i, i + 1) for i in range(PATCHES - 1)]
    )
    below = lax.ppermute(
        stale_edges[:, 0].transpose(0, 2, 1), patch, [(i + 1, i) for i in range(PATCHES - 1)]
    )
    tokens = call(tokens_kernel, (4 * COLS, TAPS_PAD), 10**6)(
        above, features[:, 0].transpose(0, 2, 1), below
    )
    sibling = lax.ppermute(tokens, "c", [(0, 1), (1, 0)])
    outgoing = call(conv_kernel, (16, 16, 2 * CH), 10**9)(tokens, sibling, weight, slot_bias, sel)
    owned = lax.all_to_all(outgoing, frame, 0, 0, tiled=True)
    done = call(
        block_kernel,
        (8, 2, 16, 2 * CH),
        2 * 10**9,
        [pltpu.VMEM((2, 5, 128, 128), jnp.float32), pltpu.VMEM((512, CH), jnp.bfloat16)],
    )(
        owned,
        jnp.asarray(channel_order(), jnp.bfloat16),
        jnp.asarray(position_rows()),
        first_gain[None],
        first_shift[None],
        query_weight,
        key_weight,
        value_weight,
        out_weight,
        out_bias[None],
        second_gain[None],
        second_shift[None],
        geglu_weight,
        geglu_bias[None],
        down_weight,
        down_bias[None],
    )
    returned = lax.all_to_all(done.reshape(16, 16, 2 * CH), frame, 0, 0, tiled=True)
    result = call(finish_kernel, (4, CH, COLS), 10**6)(returned)
    return result.transpose(0, 2, 1)[:, None]


def solution(mesh):
    split = Mesh(mesh.devices.reshape(4, 2, 2, 4, 8), ("x", "yh", "c", "yl", "z"))
    frame, patch = ("x", "yh", "c"), ("yl", "z")
    return jax.shard_map(
        per_device,
        mesh=split,
        in_specs=(P(frame, patch), P(frame, patch), P(None, None, None, frame)) + (P(),) * 14,
        out_specs=P(frame, patch),
        check_vma=False,
    )
```

time: 221 us -> 100 us (0.45)
  the two profiles are of different devices: /device:TPU:17 before, /device:TPU:9 now
where the time goes in v1:
time: 100 us; the launch traced here: 99.7 us
  starting transfers between devices  36 us (36%)
  waiting for transfers between devices  22.6 us (23%)
  blocking collectives  19.3 us (19%)
  Pallas kernels  13 us (13%)
  local copies, waits for them, and re-layouts  7.82 us (8%)
    all_to_all x1, blocking collectives, per_device(): lax.all_to_all(done.reshape(16, 16, 2 * CH), frame, 0, 0, tiled=True)  19.3 us
    all_to_all x1, waiting for transfers between devices, per_device(): owned = lax.all_to_all(outgoing, frame, 0, 0, tiled=True)  13.3 us
    ppermute x3, starting transfers between devices, per_device(): lax.ppermute(pair, 'x', [((x + j) % 4, x) for x in range(4)])  9.33 us
    ppermute x3, waiting for transfers between devices, per_device(): lax.ppermute(pair, 'x', [((x + j) % 4, x) for x in range(4)])  9.25 us
    pallas_call x1, Pallas kernels, per_device(): call(block_kernel, (8, 2, 16, 2 * CH), 2 * 10 ** 9, [pltpu.VMEM((2, 5, 12...  8.76 us
    ppermute x1, starting transfers between devices, per_device(): lax.ppermute(stale_edges[:, 0].transpose(0, 2, 1), patch, [(i + 1, i) for...  7.8 us
    unnamed x39, local copies, waits for them, and re-layouts  6.31 us
    ppermute x1, starting transfers between devices, per_device(): other = lax.ppermute(packed, ('yh', 'yl'), mirrored)  5.9 us
  transfers between devices with their start and end apart: 8, of which 3 were waited for; matrix products, arithmetic and copies ran while one was open for 4% of the time, Pallas kernels for 0%

profile of v1, /device:TPU:9, one launch (start us, length us, event | category | flops | bytes accessed | tf_op | source)
XLA Modules:
  0.0 99.7 jit_solution(9306136257823336254)
XLA Ops:
  0.0 0.9 copy-done.1
  1.0 5.9 %collective-permute-start.3 = (bf16[24,3072]{1,0:T(8,128)(2,1)S(1)}, bf16[24,3072]{1,0:T(8,128)(2,1)S(1)}, u32[]{:S(2)}, u32[]{:S(2)}) collective-permute-start(bf16[24,3072]{1,0:T(8,128)(2,1)S(1)} %shard_map.182), channel_id=1, source_target_pairs={{0,88},{8,80},{16,72},{24,64},{64,24},{72,16},{80,8},{88,0},{1,89}... | collective-permute-start | bytes 442376 | tf_op jit(solution)/shard_map/ppermute | solution.py:259
  6.9 1.1 %slice_bitcast_fusion = (bf16[4,320,128]{2,1,0:T(8,128)(2,1)S(1)}, bf16[4,320,128]{2,1,0:T(8,128)(2,1)S(1)}) fusion(bf16[4,2,128,320]{2,3,1,0:T(8,128)(2,1)} %param.20), kind=kLoop, calls=%fused_computation | loop fusion | bytes 1310720 | tf_op jit(solution)/shard_map/transpose | solution.py:278
  8.1 4.0 %collective-permute-start = (bf16[4,320,128]{2,1,0:T(8,128)(2,1)S(1)}, bf16[4,320,128]{2,1,0:T(8,128)(2,1)S(1)}, u32[]{:S(2)}, u32[]{:S(2)}) collective-permute-start(bf16[4,320,128]{2,1,0:T(8,128)(2,1)S(1)} %get-tuple-element.6), channel_id=1, source_target_pairs={{0,1},{1,2},{2,3},{3,4},{4,5},{5,6},{6,7},{7,8},{8,9},{9,10},{10,1... | collective-permute-start | bytes 983048 | tf_op jit(solution)/shard_map/ppermute | solution.py:274
  12.1 7.8 %collective-permute-start.1 = (bf16[4,320,128]{2,1,0:T(8,128)(2,1)S(1)}, bf16[4,320,128]{2,1,0:T(8,128)(2,1)S(1)}, u32[]{:S(2)}, u32[]{:S(2)}) collective-permute-start(bf16[4,320,128]{2,1,0:T(8,128)(2,1)S(1)} %get-tuple-element.5), channel_id=1, source_target_pairs={{1,0},{2,1},{3,2},{4,3},{5,4},{6,5},{7,6},{8,7},{9,8},{10,9},{11,1... | collective-permute-start | bytes 983048 | tf_op jit(solution)/shard_map/ppermute | solution.py:277
  20.5 0.2 select_reduce_fusion
  20.8 4.4 %collective-permute-start.4 = (bf16[2,24,3072]{2,1,0:T(8,128)(2,1)S(1)}, bf16[2,24,3072]{2,1,0:T(8,128)(2,1)S(1)}, u32[]{:S(2)}, u32[]{:S(2)}) collective-permute-start(bf16[2,24,3072]{2,1,0:T(8,128)(2,1)S(1)} %pad_maximum_fusion), channel_id=1, source_target_pairs={{128,0},{256,128},{384,256},{0,384},{129,1},{257,129},{385,257},{1... | collective-permute-start | bytes 884744 | tf_op jit(solution)/shard_map/ppermute | solution.py:262
  25.2 2.4 %collective-permute-start.5 = (bf16[2,24,3072]{2,1,0:T(8,128)(2,1)S(1)}, bf16[2,24,3072]{2,1,0:T(8,128)(2,1)S(1)}, u32[]{:S(2)}, u32[]{:S(2)}) collective-permute-start(bf16[2,24,3072]{2,1,0:T(8,128)(2,1)S(1)} %pad_maximum_fusion), channel_id=1, source_target_pairs={{256,0},{384,128},{0,256},{128,384},{257,1},{385,129},{1,257},{129... | collective-permute-start | bytes 884744 | tf_op jit(solution)/shard_map/ppermute | solution.py:262
  27.6 2.5 %collective-permute-start.6 = (bf16[2,24,3072]{2,1,0:T(8,128)(2,1)S(1)}, bf16[2,24,3072]{2,1,0:T(8,128)(2,1)S(1)}, u32[]{:S(2)}, u32[]{:S(2)}) collective-permute-start(bf16[2,24,3072]{2,1,0:T(8,128)(2,1)S(1)} %pad_maximum_fusion), channel_id=1, source_target_pairs={{384,0},{0,128},{128,256},{256,384},{385,1},{1,129},{129,257},{257... | collective-permute-start | bytes 884744 | tf_op jit(solution)/shard_map/ppermute | solution.py:262
  30.2 0.3 shard_map.181.x_ref
  30.5 4.0 %collective-permute-start.2 = (bf16[512,1024]{1,0:T(8,128)(2,1)S(1)}, bf16[512,1024]{1,0:T(8,128)(2,1)S(1)}, u32[]{:S(2)}, u32[]{:S(2)}) collective-permute-start(bf16[512,1024]{1,0:T(8,128)(2,1)S(1)} %shard_map.181.x_ref), channel_id=1, source_target_pairs={{0,32},{32,0},{1,33},{33,1},{2,34},{34,2},{3,35},{35,3},{4,36},{36... | collective-permute-start | bytes 3145736 | tf_op jit(solution)/shard_map/ppermute | solution.py:283
  34.6 1.1 %collective-permute-done.5 = bf16[2,24,3072]{2,1,0:T(8,128)(2,1)S(1)} collective-permute-done((bf16[2,24,3072]{2,1,0:T(8,128)(2,1)S(1)}, bf16[2,24,3072]{2,1,0:T(8,128)(2,1)S(1)}, u32[]{:S(2)}, u32[]{:S(2)}) %collective-permute-start.5) | collective-permute-done | bytes 294944 | tf_op jit(solution)/shard_map/ppermute | solution.py:262
  35.6 8.2 %collective-permute-done.6 = bf16[2,24,3072]{2,1,0:T(8,128)(2,1)S(1)} collective-permute-done((bf16[2,24,3072]{2,1,0:T(8,128)(2,1)S(1)}, bf16[2,24,3072]{2,1,0:T(8,128)(2,1)S(1)}, u32[]{:S(2)}, u32[]{:S(2)}) %collective-permute-start.6) | collective-permute-done | bytes 294944 | tf_op jit(solution)/shard_map/ppermute | solution.py:262
  43.9 2.9 %shard_map.183 = bf16[16,16,640]{2,1,0:T(8,128)(2,1)} custom-call(bf16[512,1024]{1,0:T(8,128)(2,1)S(1)} %shard_map.181.x_ref, bf16[512,1024]{1,0:T(8,128)(2,1)S(1)} %collective-permute-done.2.sibling_ref, bf16[8,24,3072]{2,1,0:T(8,128)(2,1)S(1)} %constant_dynamic-update-slice_fusion.w_ref, f32[1,192]{1,0:T(1,128)S(1)} %bitcast.39, ...), custom_call_target="tpu_custom_call" | custom-call | flops 1000000000 | bytes 4194304 | tf_op jit(solution)/shard_map/pallas_call | solution.py:284
  46.8 5.0 %all-to-all-start = ((bf16[16,16,640]{2,1,0:T(8,128)(2,1)}), bf16[16,16,640]{2,1,0:T(8,128)(2,1)S(1)}, u32[]{:S(2)}, u32[]{:S(2)}) async-start(bf16[16,16,640]{2,1,0:T(8,128)(2,1)} %shard_map.183), calls=%async_computation | async-start | bytes 655360 | tf_op jit(solution)/shard_map/all_to_all | solution.py:285
  51.8 1.5 %copy.22.down_ref = bf16[1280,320]{1,0:T(8,128)(2,1)S(1)} copy(bf16[1280,320]{0,1:T(8,128)(2,1)} %param.34) | data formatting | bytes 1638400 | tf_op args[15]
  53.5 13.3 %all-to-all-done.x_ref = bf16[16,16,640]{2,1,0:T(8,128)(2,1)S(1)} async-done(((bf16[16,16,640]{2,1,0:T(8,128)(2,1)}), bf16[16,16,640]{2,1,0:T(8,128)(2,1)S(1)}, u32[]{:S(2)}, u32[]{:S(2)}) %all-to-all-start) | async-done | bytes 327712 | tf_op jit(solution)/shard_map/all_to_all | solution.py:285
  66.9 0.9 copy-done.5
  67.8 0.9 copy-done.6
  68.7 0.9 copy-done.7
  69.7 0.9 copy-done.8
  70.6 8.8 %shard_map.184 = bf16[8,2,16,640]{3,2,1,0:T(8,128)(2,1)S(1)} custom-call(bf16[16,16,640]{2,1,0:T(8,128)(2,1)S(1)} %all-to-all-done.x_ref, bf16[2,160,320]{2,1,0:T(8,128)(2,1)S(1)} %copy-done.7, f32[64,320]{1,0:T(8,128)S(1)} %copy-done.8, f32[1,320]{1,0:T(1,128)S(1)} %broadcast_in_dim.59.first_gain_ref, f32[1,320]{1,0:T(1,128)S(1)} %broadcast_in_dim.60.first_shift_ref, ...), custom_call_target="tpu_custom_call" | custom-call | flops 2000000000 | bytes 4194304 | tf_op jit(solution)/shard_map/pallas_call | solution.py:286
  79.4 19.3 %all_to_all.10.x_ref = bf16[16,16,640]{2,1,0:T(8,128)(2,1)S(1)} all-to-all(bf16[16,16,640]{2,1,0:T(8,128)(2,1)S(1)} %bitcast.37), channel_id=1, replica_groups=mesh['x'=4,'yh'=2,'c'=2,'yl'=4,'z'=8] {'x','yh','c'}, dimensions={0} | all-to-all | bytes 655360 | tf_op jit(solution)/shard_map/all_to_all | solution.py:309
  98.7 1.0 shard_map.185
  (57 shorter events, 0.9 us)
Async XLA Ops:
  0.0 0.9 copy-start.1
  0.9 19.4 %copy-start.10 = (f32[320]{0:T(512)S(1)}, f32[320]{0:T(512)}, u32[]{:S(2)}) copy-start(f32[320]{0:T(512)} %param.22) | copy-start | bytes 3844
  1.0 29.1 %copy-start = (bf16[4,1,128,320]{2,3,1,0:T(8,128)(2,1)S(1)}, bf16[4,1,128,320]{2,3,1,0:T(8,128)(2,1)}, u32[]{:S(2)}) copy-start(bf16[4,1,128,320]{2,3,1,0:T(8,128)(2,1)} %param.19) | copy-start | bytes 983044
  1.0 19.7 %collective-permute-start.3 = (bf16[24,3072]{1,0:T(8,128)(2,1)S(1)}, bf16[24,3072]{1,0:T(8,128)(2,1)S(1)}, u32[]{:S(2)}, u32[]{:S(2)}) collective-permute-start(bf16[24,3072]{1,0:T(8,128)(2,1)S(1)} %shard_map.182), channel_id=1, source_target_pairs={{0,88},{8,80},{16,72},{24,64},{64,24},{72,16},{80,8},{88,0},{1,89}... | collective-permute-start | bytes 442376 | tf_op jit(solution)/shard_map/ppermute | solution.py:259
  8.1 22.1 %collective-permute-start = (bf16[4,320,128]{2,1,0:T(8,128)(2,1)S(1)}, bf16[4,320,128]{2,1,0:T(8,128)(2,1)S(1)}, u32[]{:S(2)}, u32[]{:S(2)}) collective-permute-start(bf16[4,320,128]{2,1,0:T(8,128)(2,1)S(1)} %get-tuple-element.6), channel_id=1, source_target_pairs={{0,1},{1,2},{2,3},{3,4},{4,5},{5,6},{6,7},{7,8},{8,9},{9,10},{10,1... | collective-permute-start | bytes 983048 | tf_op jit(solution)/shard_map/ppermute | solution.py:274
  12.1 18.1 %collective-permute-start.1 = (bf16[4,320,128]{2,1,0:T(8,128)(2,1)S(1)}, bf16[4,320,128]{2,1,0:T(8,128)(2,1)S(1)}, u32[]{:S(2)}, u32[]{:S(2)}) collective-permute-start(bf16[4,320,128]{2,1,0:T(8,128)(2,1)S(1)} %get-tuple-element.5), channel_id=1, source_target_pairs={{1,0},{2,1},{3,2},{4,3},{5,4},{6,5},{7,6},{8,7},{9,8},{10,9},{11,1... | collective-permute-start | bytes 983048 | tf_op jit(solution)/shard_map/ppermute | solution.py:277
  20.8 13.7 %collective-permute-start.4 = (bf16[2,24,3072]{2,1,0:T(8,128)(2,1)S(1)}, bf16[2,24,3072]{2,1,0:T(8,128)(2,1)S(1)}, u32[]{:S(2)}, u32[]{:S(2)}) collective-permute-start(bf16[2,24,3072]{2,1,0:T(8,128)(2,1)S(1)} %pad_maximum_fusion), channel_id=1, source_target_pairs={{128,0},{256,128},{384,256},{0,384},{129,1},{257,129},{385,257},{1... | collective-permute-start | bytes 884744 | tf_op jit(solution)/shard_map/ppermute | solution.py:262
  25.2 10.4 %collective-permute-start.5 = (bf16[2,24,3072]{2,1,0:T(8,128)(2,1)S(1)}, bf16[2,24,3072]{2,1,0:T(8,128)(2,1)S(1)}, u32[]{:S(2)}, u32[]{:S(2)}) collective-permute-start(bf16[2,24,3072]{2,1,0:T(8,128)(2,1)S(1)} %pad_maximum_fusion), channel_id=1, source_target_pairs={{256,0},{384,128},{0,256},{128,384},{257,1},{385,129},{1,257},{129... | collective-permute-start | bytes 884744 | tf_op jit(solution)/shard_map/ppermute | solution.py:262
  27.6 16.2 %collective-permute-start.6 = (bf16[2,24,3072]{2,1,0:T(8,128)(2,1)S(1)}, bf16[2,24,3072]{2,1,0:T(8,128)(2,1)S(1)}, u32[]{:S(2)}, u32[]{:S(2)}) collective-permute-start(bf16[2,24,3072]{2,1,0:T(8,128)(2,1)S(1)} %pad_maximum_fusion), channel_id=1, source_target_pairs={{384,0},{0,128},{128,256},{256,384},{385,1},{1,129},{129,257},{257... | collective-permute-start | bytes 884744 | tf_op jit(solution)/shard_map/ppermute | solution.py:262
  30.5 13.3 %collective-permute-start.2 = (bf16[512,1024]{1,0:T(8,128)(2,1)S(1)}, bf16[512,1024]{1,0:T(8,128)(2,1)S(1)}, u32[]{:S(2)}, u32[]{:S(2)}) collective-permute-start(bf16[512,1024]{1,0:T(8,128)(2,1)S(1)} %shard_map.181.x_ref), channel_id=1, source_target_pairs={{0,32},{32,0},{1,33},{33,1},{2,34},{34,2},{3,35},{35,3},{4,36},{36... | collective-permute-start | bytes 3145736 | tf_op jit(solution)/shard_map/ppermute | solution.py:283
  46.7 6.6 %copy-start.9 = (f32[2560]{0:T(1024)S(1)}, f32[2560]{0:T(1024)}, u32[]{:S(2)}) copy-start(f32[2560]{0:T(1024)} %param.33) | copy-start | bytes 30724
  46.7 6.6 %copy-start.11 = (f32[320]{0:T(512)S(1)}, f32[320]{0:T(512)}, u32[]{:S(2)}) copy-start(f32[320]{0:T(512)} %param.23) | copy-start | bytes 3844
  46.7 6.7 %copy-start.12 = (f32[320]{0:T(512)S(1)}, f32[320]{0:T(512)}, u32[]{:S(2)}) copy-start(f32[320]{0:T(512)} %param.24) | copy-start | bytes 3844
  46.7 6.7 %copy-start.13 = (f32[320]{0:T(512)S(1)}, f32[320]{0:T(512)}, u32[]{:S(2)}) copy-start(f32[320]{0:T(512)} %param.29) | copy-start | bytes 3844
  46.7 6.7 %copy-start.14 = (f32[320]{0:T(512)S(1)}, f32[320]{0:T(512)}, u32[]{:S(2)}) copy-start(f32[320]{0:T(512)} %param.30) | copy-start | bytes 3844
  46.8 6.7 %copy-start.15 = (f32[320]{0:T(512)S(1)}, f32[320]{0:T(512)}, u32[]{:S(2)}) copy-start(f32[320]{0:T(512)} %param.31) | copy-start | bytes 3844
  46.8 6.7 %copy-start.16 = (f32[320]{0:T(512)S(1)}, f32[320]{0:T(512)}, u32[]{:S(2)}) copy-start(f32[320]{0:T(512)} %param.35) | copy-start | bytes 3844
  46.8 20.1 %copy-start.2 = (bf16[320,2560]{1,0:T(8,128)(2,1)S(1)}, bf16[320,2560]{1,0:T(8,128)(2,1)}, u32[]{:S(2)}) copy-start(bf16[320,2560]{1,0:T(8,128)(2,1)} %geglu_ref.1) | copy-start | bytes 4915204
  46.8 20.1 %copy-start.3 = (bf16[320,320]{1,0:T(8,128)(2,1)S(1)}, bf16[320,320]{1,0:T(8,128)(2,1)}, u32[]{:S(2)}) copy-start(bf16[320,320]{1,0:T(8,128)(2,1)} %query_ref.1) | copy-start | bytes 614404
  46.8 20.0 %copy-start.4 = (bf16[320,320]{1,0:T(8,128)(2,1)S(1)}, bf16[320,320]{1,0:T(8,128)(2,1)}, u32[]{:S(2)}) copy-start(bf16[320,320]{1,0:T(8,128)(2,1)} %key_ref.1) | copy-start | bytes 614404
  46.8 20.0 %all-to-all-start = ((bf16[16,16,640]{2,1,0:T(8,128)(2,1)}), bf16[16,16,640]{2,1,0:T(8,128)(2,1)S(1)}, u32[]{:S(2)}, u32[]{:S(2)}) async-start(bf16[16,16,640]{2,1,0:T(8,128)(2,1)} %shard_map.183), calls=%async_computation | async-start | bytes 655360 | tf_op jit(solution)/shard_map/all_to_all | solution.py:285
  66.8 0.9 copy-start.5
  67.8 0.9 copy-start.6
  68.7 0.9 copy-start.7
  (1 other events, 0.9 us)

commit v2 on v1

v2 whole, which is shorter than its diff:
```python
import functools
import math

import jax
import jax.numpy as jnp
import numpy as np
from jax import lax
from jax.experimental import pallas as pl
from jax.experimental.pallas import tpu as pltpu
from jax.sharding import Mesh, PartitionSpec as P

HEADS = 8
CH = 320
FF = 1280
TAPS_IN = 960
TAPS_PAD = 1024
SHARE = 20
PIECE = 768
FRAMES = 64
COLS = 128
PATCHES = 32
TOKENS_FLOPS = 2*10**10
MIB = 1024 * 1024


def pack_weight_kernel(w_ref, out_ref):
    blank = jnp.zeros((SHARE, TAPS_PAD - TAPS_IN), jnp.float32)
    rows = jnp.concatenate(
        [
            part
            for b in range(3)
            for part in [w_ref[a, b].astype(jnp.float32) for a in range(3)] + [blank]
        ],
        axis=1,
    )
    last = jnp.concatenate([rows[16:, q * PIECE : (q + 1) * PIECE] for q in range(4)], axis=0)
    out_ref[...] = jnp.concatenate([rows[:16], last], axis=1).astype(jnp.bfloat16)


def fan_kernel(own_ref, other_ref, place_ref, out_ref):
    y = place_ref[1]
    for x in range(4):
        out_ref[x, y] = own_ref[...]
        out_ref[x, 1 - y] = other_ref[...]


def tokens_kernel(above_ref, band_ref, below_ref, out_ref):
    blank = jnp.zeros((TAPS_PAD - TAPS_IN, COLS), jnp.bfloat16)
    for f in range(4):
        stacked = jnp.concatenate([above_ref[f], band_ref[f], below_ref[f], blank], axis=0)
        out_ref[f * COLS : (f + 1) * COLS, :] = stacked.T


def convolve(x_ref, w_ref, bias):
    x = x_ref[...]
    tokens = x.shape[0]
    position = lax.broadcasted_iota(jnp.int32, (tokens, 1), 0) % COLS
    split = w_ref[:, :, 3 * TAPS_PAD :].astype(jnp.float32)
    last = jnp.concatenate(
        [
            jnp.concatenate([split[chip, q * 4 : (q + 1) * 4] for chip in range(8)], axis=0)
            for q in range(4)
        ],
        axis=1,
    ).astype(jnp.bfloat16)

    def taps(b):
        cols = slice(b * TAPS_PAD, (b + 1) * TAPS_PAD)
        weight = jnp.concatenate([w_ref[:, :, cols].reshape(-1, TAPS_PAD), last[:, cols]], axis=0)
        return lax.dot_general(
            x, weight, (((1,), (1,)), ((), ())), preferred_element_type=jnp.float32
        )

    left = jnp.where(position == 0, 0.0, pltpu.roll(taps(0), 1, 0))
    right = jnp.where(position == COLS - 1, 0.0, pltpu.roll(taps(2), tokens - 1, 0))
    return taps(1) + left + right + bias


def conv_first_kernel(x_ref, w_ref, bias_ref, order_ref, out_ref):
    rows = convolve(x_ref, w_ref, bias_ref[:1, : CH // 2]).astype(jnp.bfloat16)
    out_ref[...] = jnp.dot(rows, order_ref[: CH // 2, :], preferred_element_type=jnp.float32)


def conv_second_kernel(x_ref, w_ref, bias_ref, order_ref, first_ref, out_ref):
    rows = convolve(x_ref, w_ref, bias_ref[1:2, : CH // 2]).astype(jnp.bfloat16)
    ordered = first_ref[...] + jnp.dot(
        rows, order_ref[CH // 2 :, :], preferred_element_type=jnp.float32
    )
    by_owner = ordered.reshape(2, 2, 16, 8, CH)
    both = jnp.concatenate([by_owner[0], by_owner[1]], axis=-1)
    for k in range(16):
        out_ref[k] = jnp.concatenate([both[0, k], both[1, k]], axis=0).astype(jnp.bfloat16)


def norm_rows(values, gain, shift):
    average = jnp.mean(values, axis=-1, keepdims=True)
    centred = values - average
    variance = jnp.mean(centred * centred, axis=-1, keepdims=True)
    return centred * lax.rsqrt(variance + 1e-05) * gain + shift


def conv_params_kernel(bias_ref, place_ref, sides_ref, order_ref):
    core = place_ref[2]
    bias = bias_ref[...]
    by_core = []
    for i in range(2):
        shares = [bias[:, (chip * 2 + i) * SHARE :][:, :SHARE] for chip in range(8)]
        by_core.append(
            jnp.concatenate([s[:, :16] for s in shares] + [s[:, 16:] for s in shares], axis=1)
        )
    sides_ref[:1, : CH // 2] = jnp.where(core == 0, by_core[0], by_core[1])
    sides_ref[1:2, : CH // 2] = jnp.where(core == 0, by_core[1], by_core[0])
    row = lax.broadcasted_iota(jnp.int32, (CH, CH), 0)
    owner = jnp.where(row < CH // 2, core, 1 - core)
    row = jnp.where(row < CH // 2, row, row - CH // 2)
    chip = jnp.where(row < 128, row >> 4, (row - 128) >> 2)
    share = jnp.where(row < 128, row & 15, 16 + (row & 3))
    channel = (chip * 2 + owner) * SHARE + share
    here = channel == lax.broadcasted_iota(jnp.int32, (CH, CH), 1)
    order_ref[...] = jnp.where(here, 1.0, 0.0).astype(jnp.bfloat16)


def block_params_kernel(*refs):
    query, key, value, out = refs[:4]
    rows = refs[4:11]
    spread_ref, square_ref, vectors_ref = refs[11:]
    source = lax.broadcasted_iota(jnp.int32, (CH, 512), 0)
    lane = lax.broadcasted_iota(jnp.int32, (CH, 512), 1)
    there = ((lane & 63) < 40) & (source == (lane >> 6) * 40 + (lane & 63))
    spread = jnp.where(there, 1.0, 0.0).astype(jnp.bfloat16)
    for i, part in enumerate((query, key)):
        spread_ref[:, i * 512 : (i + 1) * 512] = jnp.dot(
            part[...], spread, preferred_element_type=jnp.float32
        ).astype(jnp.bfloat16)
    square_ref[:CH, :] = value[...].astype(jnp.float32).T.astype(jnp.bfloat16)
    square_ref[CH:, :] = out[...]
    vectors_ref[:FRAMES, :] = rows[0][...]
    for i, row in enumerate(rows[1:]):
        vectors_ref[FRAMES + i : FRAMES + i + 1, :] = row[...]
    vectors_ref[FRAMES + 6 :, :] = jnp.zeros((2, CH), jnp.float32)


def attention_kernel(x_ref, spread_ref, square_ref, vectors_ref, middle_ref, rows_ref, context_ref):
    first_gain, first_shift, out_bias = (
        vectors_ref[FRAMES + i : FRAMES + i + 1, :] for i in range(3)
    )
    pixels = 8
    blocks = 2 * CH // 128
    received = x_ref[...].astype(jnp.float32).reshape(256, 2 * CH)
    for i in range(blocks):
        rows_ref[i] = received[:, i * 128 : (i + 1) * 128]
    pieces = []
    for p in range(pixels):
        both = jnp.concatenate(
            [rows_ref[i, pl.ds(p, 32, stride=pixels), :] for i in range(blocks)], axis=1
        )
        pieces += [both[:, :CH], both[:, CH:]]
    x = jnp.concatenate(pieces, axis=0)
    position = vectors_ref[:FRAMES, :]
    normed = norm_rows(x, first_gain, first_shift).reshape(pixels, FRAMES, CH)
    normed = (normed + position[None]).reshape(pixels * FRAMES, CH).astype(jnp.bfloat16)

    queries, key_rows = (
        jnp.dot(
            normed, spread_ref[:, i * 512 : (i + 1) * 512], preferred_element_type=jnp.float32
        ).astype(jnp.bfloat16)
        for i in range(2)
    )
    across = (((1,), (1,)), ((), ()))
    values = lax.dot_general(
        square_ref[:CH, :], normed, across, preferred_element_type=jnp.float32
    ).astype(jnp.bfloat16)
    scale = 1.0 / math.sqrt(CH // HEADS)
    head_of = lax.broadcasted_iota(jnp.int32, (1, 256), 1) >> 6
    units = [(p, quad) for p in range(pixels) for quad in range(2)]
    scores = []
    for p, quad in units:
        rows = slice(p * FRAMES, (p + 1) * FRAMES)
        lanes = slice(quad * 256, (quad + 1) * 256)
        query = queries[rows, lanes]
        stacked = jnp.concatenate(
            [jnp.where(head_of == h, query, jnp.zeros_like(query)) for h in range(4)], axis=0
        )
        scores.append(
            lax.dot_general(
                key_rows[rows, lanes], stacked, across, preferred_element_type=jnp.float32
            )
        )
    scores = jnp.concatenate(scores, axis=1)
    expo = jnp.exp((scores - jnp.max(scores, axis=0, keepdims=True)) * scale)
    probs = (expo * (1.0 / jnp.sum(expo, axis=0, keepdims=True))).astype(jnp.bfloat16)
    contexts = []
    for i, (p, quad) in enumerate(units):
        rows = slice(p * FRAMES, (p + 1) * FRAMES)
        mixed = jnp.dot(
            values[quad * 160 : (quad + 1) * 160, rows],
            probs[:, i * 256 : (i + 1) * 256],
            preferred_element_type=jnp.float32,
        )
        for h in range(4):
            contexts.append(mixed[h * 40 : (h + 1) * 40, h * FRAMES : (h + 1) * FRAMES])
    for p in range(0, pixels, 2):
        left = jnp.concatenate(contexts[p * HEADS : (p + 1) * HEADS], axis=0)
        right = jnp.concatenate(contexts[(p + 1) * HEADS : (p + 2) * HEADS], axis=0)
        context_ref[:, p * FRAMES : (p + 2) * FRAMES] = jnp.concatenate(
            [left, right], axis=1
        ).astype(jnp.bfloat16)
    attn_out = (
        lax.dot_general(
            context_ref[...],
            square_ref[CH:, :],
            (((0,), (0,)), ((), ())),
            preferred_element_type=jnp.float32,
        )
        + out_bias
    ).astype(jnp.bfloat16)
    middle_ref[...] = (x + attn_out.astype(jnp.float32)).astype(jnp.bfloat16)


def feed_kernel(middle_ref, vectors_ref, geglu_ref, geglu_bias_ref, down_ref, out_ref, rows_ref):
    pixels = 8
    blocks = 2 * CH // 128
    second_gain, second_shift, down_bias = (
        vectors_ref[FRAMES + i : FRAMES + i + 1, :] for i in range(3, 6)
    )
    middle = middle_ref[...].astype(jnp.float32)
    normed_two = norm_rows(middle, second_gain, second_shift).astype(jnp.bfloat16)
    total = middle + down_bias
    step = 256
    for start in range(0, FF, step):
        lanes = slice(start, start + step)
        gates = slice(FF + start, FF + start + step)
        value = (
            jnp.dot(normed_two, geglu_ref[:, lanes], preferred_element_type=jnp.float32)
            + geglu_bias_ref[:, lanes]
        )
        gate = (
            jnp.dot(normed_two, geglu_ref[:, gates], preferred_element_type=jnp.float32)
            + geglu_bias_ref[:, gates]
        )
        hidden = value * (0.5 * gate * (1.0 + lax.erf(gate * (1.0 / math.sqrt(2.0)))))
        total = total + lax.dot_general(
            hidden.astype(jnp.bfloat16),
            down_ref[:, lanes],
            (((1,), (1,)), ((), ())),
            preferred_element_type=jnp.float32,
        )
    for p in range(pixels):
        near = total[p * FRAMES : p * FRAMES + 32]
        far = total[p * FRAMES + 32 : (p + 1) * FRAMES]
        both = jnp.concatenate([near, far], axis=1)
        for i in range(blocks):
            rows_ref[i, pl.ds(p, 32, stride=pixels), :] = both[:, i * 128 : (i + 1) * 128]
    for i in range(blocks):
        out_ref[:, :, i * 128 : (i + 1) * 128] = (
            rows_ref[i].astype(jnp.bfloat16).reshape(16, 16, 128)
        )


def finish_kernel(x_ref, out_ref):
    received = x_ref[...].astype(jnp.float32)
    for half in range(2):
        lanes = slice(half * CH, (half + 1) * CH)
        for f in range(2):
            rows = received[:, f * 8 : (f + 1) * 8, lanes].reshape(COLS, CH)
            out_ref[half * 2 + f] = rows.T.astype(jnp.bfloat16)


def call(kernel, out_shape, flops, scratch=(), in_specs=None, vmem=8):
    many = isinstance(out_shape, list)
    shapes = [jax.ShapeDtypeStruct(*o) for o in out_shape] if many else out_shape
    spaces = {}
    if in_specs is not None:
        spaces["in_specs"] = [pl.BlockSpec(memory_space=i or pltpu.VMEM) for i in in_specs]
    return pl.pallas_call(
        kernel,
        out_shape=shapes if many else jax.ShapeDtypeStruct(out_shape, jnp.bfloat16),
        scratch_shapes=list(scratch),
        compiler_params=pltpu.CompilerParams(vmem_limit_bytes=vmem * MIB),
        cost_estimate=pl.CostEstimate(flops=flops, bytes_accessed=4 * MIB, transcendentals=0),
        **spaces,
    )


def position_rows():
    frames = np.array([d * 4 + high * 2 + low for high in range(2) for d in range(16) for low in range(2)])
    rates = 10000.0 ** (-2.0 * np.arange(CH // 2) / CH)
    angles = frames[:, None] * rates[None, :]
    return np.stack([np.sin(angles), np.cos(angles)], axis=-1).reshape(FRAMES, CH).astype(np.float32)


def per_device(
    features,
    stale_edges,
    conv_weight,
    conv_bias,
    first_gain,
    first_shift,
    query_weight,
    key_weight,
    value_weight,
    out_weight,
    out_bias,
    second_gain,
    second_shift,
    geglu_weight,
    geglu_bias,
    down_weight,
    down_bias,
):
    frame = ("x", "yh", "c")
    patch = ("yl", "z")
    packed = call(pack_weight_kernel, (16, 3 * TAPS_PAD + PIECE), 10**6)(
        conv_weight.transpose(0, 1, 3, 2)
    )
    mirrored = [(h * 4 + l, (1 - h) * 4 + 3 - l) for h in range(2) for l in range(4)]
    other = lax.ppermute(packed, ("yh", "yl"), mirrored)
    place = jnp.stack([lax.axis_index(a) for a in frame]).astype(jnp.int32)
    fanned = call(
        fan_kernel, (4, 2, 16, 3 * TAPS_PAD + PIECE), 10**6, in_specs=[None, None, pltpu.SMEM]
    )(packed, other, place)
    weight = lax.all_to_all(fanned, "x", 0, 0, tiled=True).reshape(8, 16, 3 * TAPS_PAD + PIECE)

    theirs = lax.ppermute(weight, "c", [(0, 1), (1, 0)])

    rims = stale_edges.transpose(0, 1, 3, 2)
    above = lax.ppermute(rims[:, 1], patch, [(i, i + 1) for i in range(PATCHES - 1)])
    below = lax.ppermute(rims[:, 0], patch, [(i + 1, i) for i in range(PATCHES - 1)])

    sides, order = call(
        conv_params_kernel,
        [((8, CH), jnp.float32), ((CH, CH), jnp.bfloat16)],
        10**6,
        in_specs=[None, pltpu.SMEM],
    )(conv_bias[None], place)
    tokens = call(tokens_kernel, (4 * COLS, TAPS_PAD), TOKENS_FLOPS)(
        above, features[:, 0].transpose(0, 2, 1), below
    )
    first = call(conv_first_kernel, [((512, CH), jnp.float32)], 10**9, vmem=24)(
        tokens, weight, sides, order
    )[0]
    outgoing = call(conv_second_kernel, (16, 16, 2 * CH), 10**9, vmem=24)(
        tokens, theirs, sides, order, first
    )
    owned = lax.all_to_all(outgoing, frame, 0, 0, tiled=True)
    rows = [first_gain, first_shift, out_bias, second_gain, second_shift, down_bias]
    query_weight, outgoing = lax.optimization_barrier((query_weight, outgoing))
    spread, square, vectors = call(
        block_params_kernel,
        [
            ((CH, 1024), jnp.bfloat16),
            ((2 * CH, CH), jnp.bfloat16),
            ((FRAMES + 8, CH), jnp.float32),
        ],
        10**6,
    )(
        query_weight,
        key_weight,
        value_weight,
        out_weight,
        position_rows(),
        *(row[None] for row in rows),
    )
    by_pixel = pltpu.VMEM((5, 256, 128), jnp.float32)
    middle = call(
        attention_kernel,
        (512, CH),
        10**9,
        [by_pixel, pltpu.VMEM((CH, 512), jnp.bfloat16)],
        vmem=24,
    )(owned, spread, square, vectors)
    done = call(feed_kernel, (16, 16, 2 * CH), 10**9, [by_pixel], vmem=24)(
        middle, vectors, geglu_weight, geglu_bias[None], down_weight.T
    )
    returned = lax.all_to_all(done, frame, 0, 0, tiled=True)
    result = call(finish_kernel, (4, CH, COLS), 10**6)(returned)
    return result.transpose(0, 2, 1)[:, None]


def solution(mesh):
    split = Mesh(mesh.devices.reshape(4, 2, 2, 4, 8), ("x", "yh", "c", "yl", "z"))
    frame, patch = ("x", "yh", "c"), ("yl", "z")
    return jax.shard_map(
        per_device,
        mesh=split,
        in_specs=(P(frame, patch), P(frame, patch), P(None, None, None, frame)) + (P(),) * 14,
        out_specs=P(frame, patch),
        check_vma=False,
    )
```

time: 100 us -> 90.5 us (0.905)
  local copies, waits for them, and re-layouts: 7.82 us -> 1.13 us
  waiting for transfers between devices: 22.6 us -> 18.8 us
  starting transfers between devices: 36 us -> 39.1 us
  blocking collectives: 19.3 us -> 16.7 us
    ppermute x6 -> x3, waiting for transfers between devices: 9.26 us -> 1.02 us  [the longest x1 0.9 us: per_device(): lax.ppermute(rims[:, 0], patch, [(i + 1, i) for i in range(PATCHES - 1)])]
    ppermute x6 -> x3, starting transfers between devices: 25.1 us -> 17.8 us  [the longest x1 10.1 us: per_device(): lax.ppermute(rims[:, 0], patch, [(i + 1, i) for i in range(PATCHES - 1)])]
    all_to_all x1, starting transfers between devices: 4.97 us -> 11.4 us  [per_device(): owned = lax.all_to_all(outgoing, frame, 0, 0, tiled=True)]
    unnamed x39 -> x37, local copies, waits for them, and re-layouts: 6.31 us -> 1.06 us
    all_to_all x0 -> x1, starting transfers between devices: none -> 4.1 us  [per_device(): lax.all_to_all(fanned, 'x', 0, 0, tiled=True)]
    ppermute x1, waiting for transfers between devices: 0.01 us -> 3.23 us  [per_device(): other = lax.ppermute(packed, ('yh', 'yl'), mirrored)]
    all_to_all x1, blocking collectives: 19.3 us -> 16.7 us  [per_device(): returned = lax.all_to_all(done, frame, 0, 0, tiled=True)]
    all_to_all x1, waiting for transfers between devices: 13.3 us -> 14.6 us  [per_device(): owned = lax.all_to_all(outgoing, frame, 0, 0, tiled=True)]
  transfers between devices with their start and end apart: 8 -> 6, of which waited for: 3 -> 4; matrix products, arithmetic and copies ran while one was open for 4% -> 0% of each run, Pallas kernels for 0% -> 3%
where the time goes in v2:
time: 90.5 us; the launch traced here: 90.1 us
  starting transfers between devices  39.1 us (43%)
  waiting for transfers between devices  18.8 us (21%)
  blocking collectives  16.7 us (18%)
  Pallas kernels  13.8 us (15%)
  local copies, waits for them, and re-layouts  1.13 us (1%)
    all_to_all x1, blocking collectives, per_device(): returned = lax.all_to_all(done, frame, 0, 0, tiled=True)  16.7 us
    all_to_all x1, waiting for transfers between devices, per_device(): owned = lax.all_to_all(outgoing, frame, 0, 0, tiled=True)  14.6 us
    all_to_all x1, starting transfers between devices, per_device(): owned = lax.all_to_all(outgoing, frame, 0, 0, tiled=True)  11.4 us
    ppermute x1, starting transfers between devices, per_device(): lax.ppermute(rims[:, 0], patch, [(i + 1, i) for i in range(PATCHES - 1)])  10.1 us
    ppermute x1, starting transfers between devices, per_device(): other = lax.ppermute(packed, ('yh', 'yl'), mirrored)  5.9 us
    all_to_all x1, starting transfers between devices, per_device(): lax.all_to_all(fanned, 'x', 0, 0, tiled=True)  4.1 us
    ppermute x1, starting transfers between devices, per_device(): lax.ppermute(rims[:, 1], patch, [(i, i + 1) for i in range(PATCHES - 1)])  4 us
    ppermute x1, starting transfers between devices, per_device(): theirs = lax.ppermute(weight, 'c', [(0, 1), (1, 0)])  3.7 us
  transfers between devices with their start and end apart: 6, of which 4 were waited for; matrix products, arithmetic and copies ran while one was open for 0% of the time, Pallas kernels for 3%

profile of v2, /device:TPU:9, one launch (start us, length us, event | category | flops | bytes accessed | tf_op | source)
XLA Modules:
  0.0 90.1 jit_solution(1666289871374911684)
XLA Ops:
  0.0 0.9 %copy-done.4 = bf16[3,3,320,20]{2,3,1,0:T(8,128)(2,1)S(1)} copy-done((bf16[3,3,320,20]{2,3,1,0:T(8,128)(2,1)S(1)}, bf16[3,3,320,20]{2,3,1,0:T(8,128)(2,1)}, u32[]{:S(2)}) %copy-start.4) | copy-done | bytes 115224
  0.9 0.1 shard_map.173.own_ref
  1.0 5.9 %collective-permute-start.2 = (bf16[16,3840]{1,0:T(8,128)(2,1)S(1)}, bf16[16,3840]{1,0:T(8,128)(2,1)S(1)}, u32[]{:S(2)}, u32[]{:S(2)}) collective-permute-start(bf16[16,3840]{1,0:T(8,128)(2,1)S(1)} %shard_map.173.own_ref), channel_id=1, source_target_pairs={{0,88},{8,80},{16,72},{24,64},{64,24},{72,16},{80,8},{88,0},{1,89}... | collective-permute-start | bytes 368648 | tf_op jit(solution)/shard_map/ppermute | solution.py:317
  6.9 0.1 pad_add_fusion.place_ref
  7.0 3.2 %collective-permute-done.2.other_ref = bf16[16,3840]{1,0:T(8,128)(2,1)S(1)} collective-permute-done((bf16[16,3840]{1,0:T(8,128)(2,1)S(1)}, bf16[16,3840]{1,0:T(8,128)(2,1)S(1)}, u32[]{:S(2)}, u32[]{:S(2)}) %collective-permute-start.2) | collective-permute-done | bytes 122912 | tf_op jit(solution)/shard_map/ppermute | solution.py:317
  10.2 1.6 %shard_map.174 = bf16[4,2,16,3840]{3,2,1,0:T(8,128)(2,1)} custom-call(bf16[16,3840]{1,0:T(8,128)(2,1)S(1)} %shard_map.173.own_ref, bf16[16,3840]{1,0:T(8,128)(2,1)S(1)} %collective-permute-done.2.other_ref, s32[3]{0:T(128)S(1)} %pad_add_fusion.place_ref), custom_call_target="tpu_custom_call" | custom-call | flops 1000000 | bytes 4194304 | tf_op jit(solution)/shard_map/pallas_call | solution.py:319
  11.8 4.1 %all-to-all-start = ((bf16[4,2,16,3840]{3,2,1,0:T(8,128)(2,1)}), bf16[4,2,16,3840]{3,2,1,0:T(8,128)(2,1)S(1)}, u32[]{:S(2)}, u32[]{:S(2)}) async-start(bf16[4,2,16,3840]{3,2,1,0:T(8,128)(2,1)} %shard_map.174), calls=%async_computation | async-start | bytes 1966080 | tf_op jit(solution)/shard_map/all_to_all | solution.py:322
  16.0 4.0 %collective-permute-start = (bf16[4,320,128]{2,1,0:T(8,128)(2,1)S(1)}, bf16[4,320,128]{2,1,0:T(8,128)(2,1)S(1)}, u32[]{:S(2)}, u32[]{:S(2)}) collective-permute-start(bf16[4,320,128]{2,1,0:T(8,128)(2,1)S(1)} %get-tuple-element.18), channel_id=1, source_target_pairs={{0,1},{1,2},{2,3},{3,4},{4,5},{5,6},{6,7},{7,8},{8,9},{9,10},{10,1... | collective-permute-start | bytes 983048 | tf_op jit(solution)/shard_map/ppermute | solution.py:327
  20.1 10.1 %collective-permute-start.1 = (bf16[4,320,128]{2,1,0:T(8,128)(2,1)S(1)}, bf16[4,320,128]{2,1,0:T(8,128)(2,1)S(1)}, u32[]{:S(2)}, u32[]{:S(2)}) collective-permute-start(bf16[4,320,128]{2,1,0:T(8,128)(2,1)S(1)} %get-tuple-element.17), channel_id=1, source_target_pairs={{1,0},{2,1},{3,2},{4,3},{5,4},{6,5},{7,6},{8,7},{9,8},{10,9},{11,1... | collective-permute-start | bytes 983048 | tf_op jit(solution)/shard_map/ppermute | solution.py:328
  30.1 0.7 shard_map.175
  30.9 3.7 %collective-permute-start.3 = (bf16[8,16,3840]{2,1,0:T(8,128)(2,1)S(1)}, bf16[8,16,3840]{2,1,0:T(8,128)(2,1)S(1)}, u32[]{:S(2)}, u32[]{:S(2)}) collective-permute-start(bf16[8,16,3840]{2,1,0:T(8,128)(2,1)S(1)} %bitcast.21), channel_id=1, source_target_pairs={{0,32},{32,0},{1,33},{33,1},{2,34},{34,2},{3,35},{35,3},{4,36},{36... | collective-permute-start | bytes 2949128 | tf_op jit(solution)/shard_map/ppermute | solution.py:324
  34.6 0.1 collective-permute-done.above_ref
  34.7 0.9 %collective-permute-done.1.below_ref = bf16[4,320,128]{2,1,0:T(8,128)(2,1)S(1)} collective-permute-done((bf16[4,320,128]{2,1,0:T(8,128)(2,1)S(1)}, bf16[4,320,128]{2,1,0:T(8,128)(2,1)S(1)}, u32[]{:S(2)}, u32[]{:S(2)}) %collective-permute-start.1) | collective-permute-done | bytes 327712 | tf_op jit(solution)/shard_map/ppermute | solution.py:328
  35.6 0.3 shard_map.172.x_ref
  35.9 1.4 %shard_map.176.first_ref = f32[512,320]{1,0:T(8,128)S(1)} custom-call(bf16[512,1024]{1,0:T(8,128)(2,1)S(1)} %shard_map.172.x_ref, bf16[8,16,3840]{2,1,0:T(8,128)(2,1)S(1)} %bitcast.22, f32[8,320]{1,0:T(8,128)S(1)} %get-tuple-element.11.bias_ref, bf16[320,320]{1,0:T(8,128)(2,1)S(1)} %get-tuple-element.12.order_ref), custom_call_target="tpu_custom_call" | custom-call | flops 1000000000 | bytes 4194304 | tf_op jit(solution)/shard_map/pallas_call | solution.py:339
  37.5 0.0 copy-start.5
  37.5 2.2 %shard_map.177 = bf16[16,16,640]{2,1,0:T(8,128)(2,1)} custom-call(bf16[512,1024]{1,0:T(8,128)(2,1)S(1)} %shard_map.172.x_ref, bf16[8,16,3840]{2,1,0:T(8,128)(2,1)S(1)} %collective-permute-done.3.w_ref, f32[8,320]{1,0:T(8,128)S(1)} %get-tuple-element.11.bias_ref, bf16[320,320]{1,0:T(8,128)(2,1)S(1)} %get-tuple-element.12.order_ref, ...), custom_call_target="tpu_custom_call" | custom-call | flops 1000000000 | bytes 4194304 | tf_op jit(solution)/shard_map/pallas_call | solution.py:342
  39.7 11.4 %all-to-all-start.1 = ((bf16[16,16,640]{2,1,0:T(8,128)(2,1)}), bf16[16,16,640]{2,1,0:T(8,128)(2,1)S(1)}, u32[]{:S(2)}, u32[]{:S(2)}) async-start(bf16[16,16,640]{2,1,0:T(8,128)(2,1)} %shard_map.177), calls=%async_computation.1 | async-start | bytes 655360 | tf_op jit(solution)/shard_map/all_to_all | solution.py:345
  51.3 0.5 shard_map.178
  51.8 14.6 %all-to-all-done.1.x_ref = bf16[16,16,640]{2,1,0:T(8,128)(2,1)S(1)} async-done(((bf16[16,16,640]{2,1,0:T(8,128)(2,1)}), bf16[16,16,640]{2,1,0:T(8,128)(2,1)S(1)}, u32[]{:S(2)}, u32[]{:S(2)}) %all-to-all-start.1) | async-done | bytes 327712 | tf_op jit(solution)/shard_map/all_to_all | solution.py:345
  66.3 3.4 %shard_map.179.middle_ref = bf16[512,320]{1,0:T(8,128)(2,1)S(1)} custom-call(bf16[16,16,640]{2,1,0:T(8,128)(2,1)S(1)} %all-to-all-done.1.x_ref, bf16[320,1024]{1,0:T(8,128)(2,1)S(1)} %get-tuple-element.14.spread_ref, bf16[640,320]{1,0:T(8,128)(2,1)S(1)} %get-tuple-element.15.square_ref, f32[72,320]{1,0:T(8,128)S(1)} %get-tuple-element.16.vectors_ref), custom_call_target="tpu_custom_call" | custom-call | flops 1000000000 | bytes 4194304 | tf_op jit(solution)/shard_map/pallas_call | solution.py:365
  69.8 2.6 %shard_map.180 = bf16[16,16,640]{2,1,0:T(8,128)(2,1)S(1)} custom-call(bf16[512,320]{1,0:T(8,128)(2,1)S(1)} %shard_map.179.middle_ref, f32[72,320]{1,0:T(8,128)S(1)} %get-tuple-element.16.vectors_ref, bf16[320,2560]{1,0:T(8,128)(2,1)S(1)} %copy-done.6, f32[1,2560]{1,0:T(1,128)S(1)} %broadcast_in_dim.34.geglu_bias_ref, bf16[320,1280]{1,0:T(8,128)(2,1)S(1)} %bitcast.24), custom_call_target="tpu_custom_call" | custom-call | flops 1000000000 | bytes 4194304 | tf_op jit(solution)/shard_map/pallas_call | solution.py:372
  72.4 16.7 %all_to_all.15.x_ref = bf16[16,16,640]{2,1,0:T(8,128)(2,1)S(1)} all-to-all(bf16[16,16,640]{2,1,0:T(8,128)(2,1)S(1)} %shard_map.180), channel_id=1, replica_groups=mesh['x'=4,'yh'=2,'c'=2,'yl'=4,'z'=8] {'x','yh','c'}, dimensions={0} | all-to-all | bytes 655360 | tf_op jit(solution)/shard_map/all_to_all | solution.py:375
  89.1 1.0 %shard_map.181 = bf16[4,320,128]{2,1,0:T(8,128)(2,1)} custom-call(bf16[16,16,640]{2,1,0:T(8,128)(2,1)S(1)} %all_to_all.15.x_ref), custom_call_target="tpu_custom_call" | custom-call | flops 1000000 | bytes 4194304 | tf_op jit(solution)/shard_map/pallas_call | solution.py:376
  (46 shorter events, 0.2 us)
Async XLA Ops:
  0.0 0.9 %copy-start.4 = (bf16[3,3,320,20]{2,3,1,0:T(8,128)(2,1)S(1)}, bf16[3,3,320,20]{2,3,1,0:T(8,128)(2,1)}, u32[]{:S(2)}) copy-start(bf16[3,3,320,20]{2,3,1,0:T(8,128)(2,1)} %param.20) | copy-start | bytes 345604
  1.0 14.9 %copy-start.9 = (bf16[4,2,128,320]{2,3,1,0:T(8,128)(2,1)S(1)}, bf16[4,2,128,320]{2,3,1,0:T(8,128)(2,1)}, u32[]{:S(2)}) copy-start(bf16[4,2,128,320]{2,3,1,0:T(8,128)(2,1)} %param.19) | copy-start | bytes 1966084
  1.0 9.2 %collective-permute-start.2 = (bf16[16,3840]{1,0:T(8,128)(2,1)S(1)}, bf16[16,3840]{1,0:T(8,128)(2,1)S(1)}, u32[]{:S(2)}, u32[]{:S(2)}) collective-permute-start(bf16[16,3840]{1,0:T(8,128)(2,1)S(1)} %shard_map.173.own_ref), channel_id=1, source_target_pairs={{0,88},{8,80},{16,72},{24,64},{64,24},{72,16},{80,8},{88,0},{1,89}... | collective-permute-start | bytes 368648 | tf_op jit(solution)/shard_map/ppermute | solution.py:317
  11.8 19.0 %all-to-all-start = ((bf16[4,2,16,3840]{3,2,1,0:T(8,128)(2,1)}), bf16[4,2,16,3840]{3,2,1,0:T(8,128)(2,1)S(1)}, u32[]{:S(2)}, u32[]{:S(2)}) async-start(bf16[4,2,16,3840]{3,2,1,0:T(8,128)(2,1)} %shard_map.174), calls=%async_computation | async-start | bytes 1966080 | tf_op jit(solution)/shard_map/all_to_all | solution.py:322
  15.9 14.2 %copy-start.11 = (f32[320]{0:T(512)S(1)}, f32[320]{0:T(512)}, u32[]{:S(2)}) copy-start(f32[320]{0:T(512)} %param.21) | copy-start | bytes 3844
  15.9 19.7 %copy-start.8 = (bf16[4,1,128,320]{2,3,1,0:T(8,128)(2,1)S(1)}, bf16[4,1,128,320]{2,3,1,0:T(8,128)(2,1)}, u32[]{:S(2)}) copy-start(bf16[4,1,128,320]{2,3,1,0:T(8,128)(2,1)} %param.18) | copy-start | bytes 983044
  16.0 18.7 %collective-permute-start = (bf16[4,320,128]{2,1,0:T(8,128)(2,1)S(1)}, bf16[4,320,128]{2,1,0:T(8,128)(2,1)S(1)}, u32[]{:S(2)}, u32[]{:S(2)}) collective-permute-start(bf16[4,320,128]{2,1,0:T(8,128)(2,1)S(1)} %get-tuple-element.18), channel_id=1, source_target_pairs={{0,1},{1,2},{2,3},{3,4},{4,5},{5,6},{6,7},{7,8},{8,9},{9,10},{10,1... | collective-permute-start | bytes 983048 | tf_op jit(solution)/shard_map/ppermute | solution.py:327
  20.1 15.5 %collective-permute-start.1 = (bf16[4,320,128]{2,1,0:T(8,128)(2,1)S(1)}, bf16[4,320,128]{2,1,0:T(8,128)(2,1)S(1)}, u32[]{:S(2)}, u32[]{:S(2)}) collective-permute-start(bf16[4,320,128]{2,1,0:T(8,128)(2,1)S(1)} %get-tuple-element.17), channel_id=1, source_target_pairs={{1,0},{2,1},{3,2},{4,3},{5,4},{6,5},{7,6},{8,7},{9,8},{10,9},{11,1... | collective-permute-start | bytes 983048 | tf_op jit(solution)/shard_map/ppermute | solution.py:328
  30.9 6.6 %collective-permute-start.3 = (bf16[8,16,3840]{2,1,0:T(8,128)(2,1)S(1)}, bf16[8,16,3840]{2,1,0:T(8,128)(2,1)S(1)}, u32[]{:S(2)}, u32[]{:S(2)}) collective-permute-start(bf16[8,16,3840]{2,1,0:T(8,128)(2,1)S(1)} %bitcast.21), channel_id=1, source_target_pairs={{0,32},{32,0},{1,33},{33,1},{2,34},{34,2},{3,35},{35,3},{4,36},{36... | collective-permute-start | bytes 2949128 | tf_op jit(solution)/shard_map/ppermute | solution.py:324
  37.3 13.7 %copy-start.12 = (f32[320]{0:T(512)S(1)}, f32[320]{0:T(512)}, u32[]{:S(2)}) copy-start(f32[320]{0:T(512)} %param.22) | copy-start | bytes 3844
  37.3 13.7 %copy-start.13 = (f32[320]{0:T(512)S(1)}, f32[320]{0:T(512)}, u32[]{:S(2)}) copy-start(f32[320]{0:T(512)} %param.23) | copy-start | bytes 3844
  37.4 13.8 %copy-start.14 = (f32[320]{0:T(512)S(1)}, f32[320]{0:T(512)}, u32[]{:S(2)}) copy-start(f32[320]{0:T(512)} %param.28) | copy-start | bytes 3844
  37.4 13.8 %copy-start.15 = (f32[320]{0:T(512)S(1)}, f32[320]{0:T(512)}, u32[]{:S(2)}) copy-start(f32[320]{0:T(512)} %param.29) | copy-start | bytes 3844
  37.4 13.8 %copy-start.16 = (f32[320]{0:T(512)S(1)}, f32[320]{0:T(512)}, u32[]{:S(2)}) copy-start(f32[320]{0:T(512)} %param.30) | copy-start | bytes 3844
  37.4 13.8 %copy-start.17 = (f32[320]{0:T(512)S(1)}, f32[320]{0:T(512)}, u32[]{:S(2)}) copy-start(f32[320]{0:T(512)} %param.34) | copy-start | bytes 3844
  37.4 13.8 %copy-start.10 = (f32[2560]{0:T(1024)S(1)}, f32[2560]{0:T(1024)}, u32[]{:S(2)}) copy-start(f32[2560]{0:T(1024)} %param.32) | copy-start | bytes 30724
  37.4 13.8 %copy-start = (bf16[320,320]{1,0:T(8,128)(2,1)S(1)}, bf16[320,320]{1,0:T(8,128)(2,1)}, u32[]{:S(2)}) copy-start(bf16[320,320]{1,0:T(8,128)(2,1)} %refs_0_) | copy-start | bytes 614404
  37.4 13.8 %copy-start.1 = (bf16[320,320]{1,0:T(8,128)(2,1)S(1)}, bf16[320,320]{1,0:T(8,128)(2,1)}, u32[]{:S(2)}) copy-start(bf16[320,320]{1,0:T(8,128)(2,1)} %refs_1_.1) | copy-start | bytes 614404
  37.4 13.8 %copy-start.2 = (bf16[320,320]{1,0:T(8,128)(2,1)S(1)}, bf16[320,320]{1,0:T(8,128)(2,1)}, u32[]{:S(2)}) copy-start(bf16[320,320]{1,0:T(8,128)(2,1)} %refs_2_.1) | copy-start | bytes 614404
  37.4 13.8 %copy-start.3 = (bf16[320,320]{1,0:T(8,128)(2,1)S(1)}, bf16[320,320]{1,0:T(8,128)(2,1)}, u32[]{:S(2)}) copy-start(bf16[320,320]{1,0:T(8,128)(2,1)} %refs_3_.1) | copy-start | bytes 614404
  37.5 13.8 %copy-start.5 = (f32[64,320]{1,0:T(8,128)S(1)}, f32[64,320]{1,0:T(8,128)}, u32[]{:S(2)}) copy-start(f32[64,320]{1,0:T(8,128)} %constant.18.clone.refs_4_) | copy-start | bytes 245764
  39.7 26.7 %all-to-all-start.1 = ((bf16[16,16,640]{2,1,0:T(8,128)(2,1)}), bf16[16,16,640]{2,1,0:T(8,128)(2,1)S(1)}, u32[]{:S(2)}, u32[]{:S(2)}) async-start(bf16[16,16,640]{2,1,0:T(8,128)(2,1)} %shard_map.177), calls=%async_computation.1 | async-start | bytes 655360 | tf_op jit(solution)/shard_map/all_to_all | solution.py:345
  66.3 3.4 %copy-start.6 = (bf16[320,2560]{1,0:T(8,128)(2,1)S(1)}, bf16[320,2560]{1,0:T(8,128)(2,1)}, u32[]{:S(2)}) copy-start(bf16[320,2560]{1,0:T(8,128)(2,1)} %geglu_ref.1) | copy-start | bytes 4915204
  66.3 3.4 %copy-start.7 = (bf16[1280,320]{0,1:T(8,128)(2,1)S(1)}, bf16[1280,320]{0,1:T(8,128)(2,1)}, u32[]{:S(2)}) copy-start(bf16[1280,320]{0,1:T(8,128)(2,1)} %param.33) | copy-start | bytes 2457604

commit v3 on v2

--- a/solution.py
+++ b/solution.py
@@ -19,7 +19,8 @@
 FRAMES = 64
 COLS = 128
 PATCHES = 32
-TOKENS_FLOPS = 2*10**10
+TOKENS_FLOPS = 5*10**9
+FAN_FLOPS = 10**6
 MIB = 1024 * 1024
 
 
@@ -44,15 +45,18 @@
         out_ref[x, 1 - y] = other_ref[...]
 
 
-def tokens_kernel(above_ref, band_ref, below_ref, out_ref):
-    blank = jnp.zeros((TAPS_PAD - TAPS_IN, COLS), jnp.bfloat16)
+def tokens_kernel(*refs):
+    *parts, out_ref = refs
     for f in range(4):
-        stacked = jnp.concatenate([above_ref[f], band_ref[f], below_ref[f], blank], axis=0)
-        out_ref[f * COLS : (f + 1) * COLS, :] = stacked.T
-
-
-def convolve(x_ref, w_ref, bias):
-    x = x_ref[...]
+        stacked = [part[f] for part in parts]
+        blank = out_ref.shape[1] - CH * len(parts)
+        if blank:
+            stacked.append(jnp.zeros((blank, COLS), jnp.bfloat16))
+        out_ref[f * COLS : (f + 1) * COLS, :] = jnp.concatenate(stacked, axis=0).T
+
+
+def convolve(upper_ref, below_ref, w_ref, bias):
+    x = jnp.concatenate([upper_ref[...], below_ref[...]], axis=1)
     tokens = x.shape[0]
     position = lax.broadcasted_iota(jnp.int32, (tokens, 1), 0) % COLS
     split = w_ref[:, :, 3 * TAPS_PAD :].astype(jnp.float32)
@@ -76,13 +80,13 @@
     return taps(1) + left + right + bias
 
 
-def conv_first_kernel(x_ref, w_ref, bias_ref, order_ref, out_ref):
-    rows = convolve(x_ref, w_ref, bias_ref[:1, : CH // 2]).astype(jnp.bfloat16)
+def conv_first_kernel(upper_ref, below_ref, w_ref, bias_ref, order_ref, out_ref):
+    rows = convolve(upper_ref, below_ref, w_ref, bias_ref[:1, : CH // 2]).astype(jnp.bfloat16)
     out_ref[...] = jnp.dot(rows, order_ref[: CH // 2, :], preferred_element_type=jnp.float32)
 
 
-def conv_second_kernel(x_ref, w_ref, bias_ref, order_ref, first_ref, out_ref):
-    rows = convolve(x_ref, w_ref, bias_ref[1:2, : CH // 2]).astype(jnp.bfloat16)
+def conv_second_kernel(upper_ref, below_ref, w_ref, bias_ref, order_ref, first_ref, out_ref):
+    rows = convolve(upper_ref, below_ref, w_ref, bias_ref[1:2, : CH // 2]).astype(jnp.bfloat16)
     ordered = first_ref[...] + jnp.dot(
         rows, order_ref[CH // 2 :, :], preferred_element_type=jnp.float32
     )
@@ -317,11 +321,9 @@
     other = lax.ppermute(packed, ("yh", "yl"), mirrored)
     place = jnp.stack([lax.axis_index(a) for a in frame]).astype(jnp.int32)
     fanned = call(
-        fan_kernel, (4, 2, 16, 3 * TAPS_PAD + PIECE), 10**6, in_specs=[None, None, pltpu.SMEM]
+        fan_kernel, (4, 2, 16, 3 * TAPS_PAD + PIECE), FAN_FLOPS, in_specs=[None, None, pltpu.SMEM]
     )(packed, other, place)
     weight = lax.all_to_all(fanned, "x", 0, 0, tiled=True).reshape(8, 16, 3 * TAPS_PAD + PIECE)
-
-    theirs = lax.ppermute(weight, "c", [(0, 1), (1, 0)])
 
     rims = stale_edges.transpose(0, 1, 3, 2)
     above = lax.ppermute(rims[:, 1], patch, [(i, i + 1) for i in range(PATCHES - 1)])
@@ -333,14 +335,16 @@
         10**6,
         in_specs=[None, pltpu.SMEM],
     )(conv_bias[None], place)
-    tokens = call(tokens_kernel, (4 * COLS, TAPS_PAD), TOKENS_FLOPS)(
-        above, features[:, 0].transpose(0, 2, 1), below
-    )
+    band = features[:, 0].transpose(0, 2, 1)
+    upper = call(tokens_kernel, (4 * COLS, 2 * CH), TOKENS_FLOPS)(above, band)
+    under = call(tokens_kernel, (4 * COLS, TAPS_PAD - 2 * CH), 12*10**9)(below)
+    weight, upper = lax.optimization_barrier((weight, upper))
+    theirs = lax.ppermute(weight, "c", [(0, 1), (1, 0)])
     first = call(conv_first_kernel, [((512, CH), jnp.float32)], 10**9, vmem=24)(
-        tokens, weight, sides, order
+        upper, under, weight, sides, order
     )[0]
     outgoing = call(conv_second_kernel, (16, 16, 2 * CH), 10**9, vmem=24)(
-        tokens, theirs, sides, order, first
+        upper, under, theirs, sides, order, first
     )
     owned = lax.all_to_all(outgoing, frame, 0, 0, tiled=True)
     rows = [first_gain, first_shift, out_bias, second_gain, second_shift, down_bias]

time: 90.5 us -> 88.2 us (0.975)
  waiting for transfers between devices: 18.8 us -> 16.8 us
  starting transfers between devices: 39.1 us -> 37.6 us
  local copies, waits for them, and re-layouts: 1.13 us -> 2.22 us
    ppermute x1, waiting for transfers between devices: 3.23 us -> 0.01 us  [per_device(): other = lax.ppermute(packed, ('yh', 'yl'), mirrored)]
    all_to_all x1, starting transfers between devices: 11.4 us -> 9.28 us  [per_device(): owned = lax.all_to_all(outgoing, frame, 0, 0, tiled=True)]
    all_to_all x1, waiting for transfers between devices: 0.01 us -> 1.82 us  [per_device(): lax.all_to_all(fanned, 'x', 0, 0, tiled=True)]
    unnamed x37 -> x35, local copies, waits for them, and re-layouts: 1.06 us -> 2.15 us
    pallas_call x2 -> x3, Pallas kernels: 1.91 us -> 1.96 us  [the longest x1 1.59 us: per_device(): call(fan_kernel, (4, 2, 16, 3 * TAPS_PAD + PIECE), FAN_FLOPS, in_specs=[N...]
  transfers between devices with their start and end apart: 6 -> 6, of which waited for: 4 -> 3; matrix products, arithmetic and copies ran while one was open for 0% -> 1% of each run, Pallas kernels for 3% -> 5%
where the time goes in v3:
time: 88.2 us; the launch traced here: 87.8 us
  starting transfers between devices  37.6 us (43%)
  waiting for transfers between devices  16.8 us (19%)
  blocking collectives  16.7 us (19%)
  Pallas kernels  13.9 us (16%)
  local copies, waits for them, and re-layouts  2.22 us (3%)
    all_to_all x1, blocking collectives, per_device(): returned = lax.all_to_all(done, frame, 0, 0, tiled=True)  16.7 us
    all_to_all x1, waiting for transfers between devices, per_device(): owned = lax.all_to_all(outgoing, frame, 0, 0, tiled=True)  14.5 us
    ppermute x1, starting transfers between devices, per_device(): lax.ppermute(rims[:, 0], patch, [(i + 1, i) for i in range(PATCHES - 1)])  10.1 us
    all_to_all x1, starting transfers between devices, per_device(): owned = lax.all_to_all(outgoing, frame, 0, 0, tiled=True)  9.28 us
    ppermute x1, starting transfers between devices, per_device(): other = lax.ppermute(packed, ('yh', 'yl'), mirrored)  5.77 us
    ppermute x1, starting transfers between devices, per_device(): theirs = lax.ppermute(weight, 'c', [(0, 1), (1, 0)])  4.34 us
    ppermute x1, starting transfers between devices, per_device(): lax.ppermute(rims[:, 1], patch, [(i, i + 1) for i in range(PATCHES - 1)])  4.13 us
    all_to_all x1, starting transfers between devices, per_device(): lax.all_to_all(fanned, 'x', 0, 0, tiled=True)  4.01 us
  transfers between devices with their start and end apart: 6, of which 3 were waited for; matrix products, arithmetic and copies ran while one was open for 1% of the time, Pallas kernels for 5%

profile of v3, /device:TPU:9, one launch (start us, length us, event | category | flops | bytes accessed | tf_op | source)
XLA Modules:
  0.0 87.8 jit_solution(4952586804540208936)
XLA Ops:
  0.0 0.9 %copy-done.4 = bf16[3,3,320,20]{2,3,1,0:T(8,128)(2,1)S(1)} copy-done((bf16[3,3,320,20]{2,3,1,0:T(8,128)(2,1)S(1)}, bf16[3,3,320,20]{2,3,1,0:T(8,128)(2,1)}, u32[]{:S(2)}) %copy-start.4) | copy-done | bytes 115224
  0.9 0.1 shard_map.172.own_ref
  1.0 5.8 %collective-permute-start = (bf16[16,3840]{1,0:T(8,128)(2,1)S(1)}, bf16[16,3840]{1,0:T(8,128)(2,1)S(1)}, u32[]{:S(2)}, u32[]{:S(2)}) collective-permute-start(bf16[16,3840]{1,0:T(8,128)(2,1)S(1)} %shard_map.172.own_ref), channel_id=1, source_target_pairs={{0,88},{8,80},{16,72},{24,64},{64,24},{72,16},{80,8},{88,0},{1,89}... | collective-permute-start | bytes 368648 | tf_op jit(solution)/shard_map/ppermute | solution.py:321
  6.8 1.1 %copy.22 = bf16[4,2,128,320]{2,3,0,1:T(8,128)(2,1)S(1)} copy(bf16[4,2,128,320]{2,3,1,0:T(8,128)(2,1)} %param.19) | data formatting | bytes 1310720 | tf_op args[1]
  8.0 4.1 %collective-permute-start.1 = (bf16[4,320,128]{2,1,0:T(8,128)(2,1)S(1)}, bf16[4,320,128]{2,1,0:T(8,128)(2,1)S(1)}, u32[]{:S(2)}, u32[]{:S(2)}) collective-permute-start(bf16[4,320,128]{2,1,0:T(8,128)(2,1)S(1)} %get-tuple-element.22), channel_id=1, source_target_pairs={{0,1},{1,2},{2,3},{3,4},{4,5},{5,6},{6,7},{7,8},{8,9},{9,10},{10,1... | collective-permute-start | bytes 983048 | tf_op jit(solution)/shard_map/ppermute | solution.py:329
  12.1 0.1 pad_add_fusion.place_ref
  12.2 1.6 %shard_map.173 = bf16[4,2,16,3840]{3,2,1,0:T(8,128)(2,1)} custom-call(bf16[16,3840]{1,0:T(8,128)(2,1)S(1)} %shard_map.172.own_ref, bf16[16,3840]{1,0:T(8,128)(2,1)S(1)} %collective-permute-done.other_ref, s32[3]{0:T(128)S(1)} %pad_add_fusion.place_ref), custom_call_target="tpu_custom_call" | custom-call | flops 1000000 | bytes 4194304 | tf_op jit(solution)/shard_map/pallas_call | solution.py:323
  13.8 4.0 %all-to-all-start = ((bf16[4,2,16,3840]{3,2,1,0:T(8,128)(2,1)}), bf16[4,2,16,3840]{3,2,1,0:T(8,128)(2,1)S(1)}, u32[]{:S(2)}, u32[]{:S(2)}) async-start(bf16[4,2,16,3840]{3,2,1,0:T(8,128)(2,1)} %shard_map.173), calls=%async_computation | async-start | bytes 1966080 | tf_op jit(solution)/shard_map/all_to_all | solution.py:326
  17.8 10.1 %collective-permute-start.2 = (bf16[4,320,128]{2,1,0:T(8,128)(2,1)S(1)}, bf16[4,320,128]{2,1,0:T(8,128)(2,1)S(1)}, u32[]{:S(2)}, u32[]{:S(2)}) collective-permute-start(bf16[4,320,128]{2,1,0:T(8,128)(2,1)S(1)} %get-tuple-element.21), channel_id=1, source_target_pairs={{1,0},{2,1},{3,2},{4,3},{5,4},{6,5},{7,6},{8,7},{9,8},{10,9},{11,1... | collective-permute-start | bytes 983048 | tf_op jit(solution)/shard_map/ppermute | solution.py:330
  27.9 0.7 shard_map.176
  28.7 0.2 shard_map.174.upper_ref
  28.9 1.8 %all-to-all-done = bf16[4,2,16,3840]{3,2,1,0:T(8,128)(2,1)S(1)} async-done(((bf16[4,2,16,3840]{3,2,1,0:T(8,128)(2,1)}), bf16[4,2,16,3840]{3,2,1,0:T(8,128)(2,1)S(1)}, u32[]{:S(2)}, u32[]{:S(2)}) %all-to-all-start) | async-done | bytes 983072 | tf_op jit(solution)/shard_map/all_to_all | solution.py:326
  30.7 4.3 %collective-permute-start.3 = (bf16[8,16,3840]{2,1,0:T(8,128)(2,1)S(1)}, bf16[8,16,3840]{2,1,0:T(8,128)(2,1)S(1)}, u32[]{:S(2)}, u32[]{:S(2)}) collective-permute-start(bf16[8,16,3840]{2,1,0:T(8,128)(2,1)S(1)} %bitcast.21), channel_id=1, source_target_pairs={{0,32},{32,0},{1,33},{33,1},{2,34},{34,2},{3,35},{35,3},{4,36},{36... | collective-permute-start | bytes 2949128 | tf_op jit(solution)/shard_map/ppermute | solution.py:342
  35.1 0.2 shard_map.175.below_ref
  35.3 1.4 %shard_map.177.first_ref = f32[512,320]{1,0:T(8,128)S(1)} custom-call(bf16[512,640]{1,0:T(8,128)(2,1)S(1)} %shard_map.174.upper_ref, bf16[512,384]{1,0:T(8,128)(2,1)S(1)} %shard_map.175.below_ref, bf16[8,16,3840]{2,1,0:T(8,128)(2,1)S(1)} %bitcast.22, f32[8,320]{1,0:T(8,128)S(1)} %get-tuple-element.15.bias_ref, bf16[320,320]{1,0:T(8,128)(2,1)S(1)} %get-tuple-element.16.order_ref), custom_call_target="tpu_custom_call" | custom-call | flops 1000000000 | bytes 4194304 | tf_op jit(solution)/shard_map/pallas_call | solution.py:343
  36.8 0.4 collective-permute-done.3.w_ref
  37.3 2.2 %shard_map.178 = bf16[16,16,640]{2,1,0:T(8,128)(2,1)} custom-call(bf16[512,640]{1,0:T(8,128)(2,1)S(1)} %shard_map.174.upper_ref, bf16[512,384]{1,0:T(8,128)(2,1)S(1)} %shard_map.175.below_ref, bf16[8,16,3840]{2,1,0:T(8,128)(2,1)S(1)} %collective-permute-done.3.w_ref, f32[8,320]{1,0:T(8,128)S(1)} %get-tuple-element.15.bias_ref, ...), custom_call_target="tpu_custom_call" | custom-call | flops 1000000000 | bytes 4194304 | tf_op jit(solution)/shard_map/pallas_call | solution.py:346
  39.4 9.3 %all-to-all-start.1 = ((bf16[16,16,640]{2,1,0:T(8,128)(2,1)}), bf16[16,16,640]{2,1,0:T(8,128)(2,1)S(1)}, u32[]{:S(2)}, u32[]{:S(2)}) async-start(bf16[16,16,640]{2,1,0:T(8,128)(2,1)} %shard_map.178), calls=%async_computation.1 | async-start | bytes 655360 | tf_op jit(solution)/shard_map/all_to_all | solution.py:349
  48.9 0.5 shard_map.179
  49.5 14.5 %all-to-all-done.1.x_ref = bf16[16,16,640]{2,1,0:T(8,128)(2,1)S(1)} async-done(((bf16[16,16,640]{2,1,0:T(8,128)(2,1)}), bf16[16,16,640]{2,1,0:T(8,128)(2,1)S(1)}, u32[]{:S(2)}, u32[]{:S(2)}) %all-to-all-start.1) | async-done | bytes 327712 | tf_op jit(solution)/shard_map/all_to_all | solution.py:349
  64.0 3.4 %shard_map.180.middle_ref = bf16[512,320]{1,0:T(8,128)(2,1)S(1)} custom-call(bf16[16,16,640]{2,1,0:T(8,128)(2,1)S(1)} %all-to-all-done.1.x_ref, bf16[320,1024]{1,0:T(8,128)(2,1)S(1)} %get-tuple-element.18.spread_ref, bf16[640,320]{1,0:T(8,128)(2,1)S(1)} %get-tuple-element.19.square_ref, f32[72,320]{1,0:T(8,128)S(1)} %get-tuple-element.20.vectors_ref), custom_call_target="tpu_custom_call" | custom-call | flops 1000000000 | bytes 4194304 | tf_op jit(solution)/shard_map/pallas_call | solution.py:369
  67.4 2.6 %shard_map.181 = bf16[16,16,640]{2,1,0:T(8,128)(2,1)S(1)} custom-call(bf16[512,320]{1,0:T(8,128)(2,1)S(1)} %shard_map.180.middle_ref, f32[72,320]{1,0:T(8,128)S(1)} %get-tuple-element.20.vectors_ref, bf16[320,2560]{1,0:T(8,128)(2,1)S(1)} %copy-done.6, f32[1,2560]{1,0:T(1,128)S(1)} %broadcast_in_dim.34.geglu_bias_ref, bf16[320,1280]{1,0:T(8,128)(2,1)S(1)} %bitcast.24), custom_call_target="tpu_custom_call" | custom-call | flops 1000000000 | bytes 4194304 | tf_op jit(solution)/shard_map/pallas_call | solution.py:376
  70.1 16.7 %all_to_all.15.x_ref = bf16[16,16,640]{2,1,0:T(8,128)(2,1)S(1)} all-to-all(bf16[16,16,640]{2,1,0:T(8,128)(2,1)S(1)} %shard_map.181), channel_id=1, replica_groups=mesh['x'=4,'yh'=2,'c'=2,'yl'=4,'z'=8] {'x','yh','c'}, dimensions={0} | all-to-all | bytes 655360 | tf_op jit(solution)/shard_map/all_to_all | solution.py:379
  86.8 1.0 %shard_map.182 = bf16[4,320,128]{2,1,0:T(8,128)(2,1)} custom-call(bf16[16,16,640]{2,1,0:T(8,128)(2,1)S(1)} %all_to_all.15.x_ref), custom_call_target="tpu_custom_call" | custom-call | flops 1000000 | bytes 4194304 | tf_op jit(solution)/shard_map/pallas_call | solution.py:380
  (45 shorter events, 0.2 us)
Async XLA Ops:
  0.0 0.9 %copy-start.4 = (bf16[3,3,320,20]{2,3,1,0:T(8,128)(2,1)S(1)}, bf16[3,3,320,20]{2,3,1,0:T(8,128)(2,1)}, u32[]{:S(2)}) copy-start(bf16[3,3,320,20]{2,3,1,0:T(8,128)(2,1)} %param.20) | copy-start | bytes 345604
  1.0 11.2 %collective-permute-start = (bf16[16,3840]{1,0:T(8,128)(2,1)S(1)}, bf16[16,3840]{1,0:T(8,128)(2,1)S(1)}, u32[]{:S(2)}, u32[]{:S(2)}) collective-permute-start(bf16[16,3840]{1,0:T(8,128)(2,1)S(1)} %shard_map.172.own_ref), channel_id=1, source_target_pairs={{0,88},{8,80},{16,72},{24,64},{64,24},{72,16},{80,8},{88,0},{1,89}... | collective-permute-start | bytes 368648 | tf_op jit(solution)/shard_map/ppermute | solution.py:321
  8.0 20.0 %copy-start.10 = (f32[320]{0:T(512)S(1)}, f32[320]{0:T(512)}, u32[]{:S(2)}) copy-start(f32[320]{0:T(512)} %param.21) | copy-start | bytes 3844
  8.0 20.7 %copy-start.8 = (bf16[4,1,128,320]{2,3,1,0:T(8,128)(2,1)S(1)}, bf16[4,1,128,320]{2,3,1,0:T(8,128)(2,1)}, u32[]{:S(2)}) copy-start(bf16[4,1,128,320]{2,3,1,0:T(8,128)(2,1)} %param.18) | copy-start | bytes 983044
  8.0 20.7 %collective-permute-start.1 = (bf16[4,320,128]{2,1,0:T(8,128)(2,1)S(1)}, bf16[4,320,128]{2,1,0:T(8,128)(2,1)S(1)}, u32[]{:S(2)}, u32[]{:S(2)}) collective-permute-start(bf16[4,320,128]{2,1,0:T(8,128)(2,1)S(1)} %get-tuple-element.22), channel_id=1, source_target_pairs={{0,1},{1,2},{2,3},{3,4},{4,5},{5,6},{6,7},{7,8},{8,9},{9,10},{10,1... | collective-permute-start | bytes 983048 | tf_op jit(solution)/shard_map/ppermute | solution.py:329
  13.8 16.9 %all-to-all-start = ((bf16[4,2,16,3840]{3,2,1,0:T(8,128)(2,1)}), bf16[4,2,16,3840]{3,2,1,0:T(8,128)(2,1)S(1)}, u32[]{:S(2)}, u32[]{:S(2)}) async-start(bf16[4,2,16,3840]{3,2,1,0:T(8,128)(2,1)} %shard_map.173), calls=%async_computation | async-start | bytes 1966080 | tf_op jit(solution)/shard_map/all_to_all | solution.py:326
  17.8 17.3 %collective-permute-start.2 = (bf16[4,320,128]{2,1,0:T(8,128)(2,1)S(1)}, bf16[4,320,128]{2,1,0:T(8,128)(2,1)S(1)}, u32[]{:S(2)}, u32[]{:S(2)}) collective-permute-start(bf16[4,320,128]{2,1,0:T(8,128)(2,1)S(1)} %get-tuple-element.21), channel_id=1, source_target_pairs={{1,0},{2,1},{3,2},{4,3},{5,4},{6,5},{7,6},{8,7},{9,8},{10,9},{11,1... | collective-permute-start | bytes 983048 | tf_op jit(solution)/shard_map/ppermute | solution.py:330
  30.7 6.5 %collective-permute-start.3 = (bf16[8,16,3840]{2,1,0:T(8,128)(2,1)S(1)}, bf16[8,16,3840]{2,1,0:T(8,128)(2,1)S(1)}, u32[]{:S(2)}, u32[]{:S(2)}) collective-permute-start(bf16[8,16,3840]{2,1,0:T(8,128)(2,1)S(1)} %bitcast.21), channel_id=1, source_target_pairs={{0,32},{32,0},{1,33},{33,1},{2,34},{34,2},{3,35},{35,3},{4,36},{36... | collective-permute-start | bytes 2949128 | tf_op jit(solution)/shard_map/ppermute | solution.py:342
  36.7 12.1 %copy-start.11 = (f32[320]{0:T(512)S(1)}, f32[320]{0:T(512)}, u32[]{:S(2)}) copy-start(f32[320]{0:T(512)} %param.22) | copy-start | bytes 3844
  36.7 12.1 %copy-start.12 = (f32[320]{0:T(512)S(1)}, f32[320]{0:T(512)}, u32[]{:S(2)}) copy-start(f32[320]{0:T(512)} %param.23) | copy-start | bytes 3844
  36.7 12.1 %copy-start.13 = (f32[320]{0:T(512)S(1)}, f32[320]{0:T(512)}, u32[]{:S(2)}) copy-start(f32[320]{0:T(512)} %param.28) | copy-start | bytes 3844
  36.7 12.1 %copy-start.14 = (f32[320]{0:T(512)S(1)}, f32[320]{0:T(512)}, u32[]{:S(2)}) copy-start(f32[320]{0:T(512)} %param.29) | copy-start | bytes 3844
  36.7 12.1 %copy-start.15 = (f32[320]{0:T(512)S(1)}, f32[320]{0:T(512)}, u32[]{:S(2)}) copy-start(f32[320]{0:T(512)} %param.30) | copy-start | bytes 3844
  36.7 12.1 %copy-start.16 = (f32[320]{0:T(512)S(1)}, f32[320]{0:T(512)}, u32[]{:S(2)}) copy-start(f32[320]{0:T(512)} %param.34) | copy-start | bytes 3844
  36.7 12.1 %copy-start.9 = (f32[2560]{0:T(1024)S(1)}, f32[2560]{0:T(1024)}, u32[]{:S(2)}) copy-start(f32[2560]{0:T(1024)} %param.32) | copy-start | bytes 30724
  36.7 12.1 %copy-start = (bf16[320,320]{1,0:T(8,128)(2,1)S(1)}, bf16[320,320]{1,0:T(8,128)(2,1)}, u32[]{:S(2)}) copy-start(bf16[320,320]{1,0:T(8,128)(2,1)} %refs_0_) | copy-start | bytes 614404
  36.8 12.1 %copy-start.1 = (bf16[320,320]{1,0:T(8,128)(2,1)S(1)}, bf16[320,320]{1,0:T(8,128)(2,1)}, u32[]{:S(2)}) copy-start(bf16[320,320]{1,0:T(8,128)(2,1)} %refs_1_.1) | copy-start | bytes 614404
  36.8 12.1 %copy-start.2 = (bf16[320,320]{1,0:T(8,128)(2,1)S(1)}, bf16[320,320]{1,0:T(8,128)(2,1)}, u32[]{:S(2)}) copy-start(bf16[320,320]{1,0:T(8,128)(2,1)} %refs_2_.1) | copy-start | bytes 614404
  36.8 12.1 %copy-start.3 = (bf16[320,320]{1,0:T(8,128)(2,1)S(1)}, bf16[320,320]{1,0:T(8,128)(2,1)}, u32[]{:S(2)}) copy-start(bf16[320,320]{1,0:T(8,128)(2,1)} %refs_3_.1) | copy-start | bytes 614404
  36.8 12.1 %copy-start.5 = (f32[64,320]{1,0:T(8,128)S(1)}, f32[64,320]{1,0:T(8,128)}, u32[]{:S(2)}) copy-start(f32[64,320]{1,0:T(8,128)} %constant.18.clone.refs_4_) | copy-start | bytes 245764
  39.4 24.6 %all-to-all-start.1 = ((bf16[16,16,640]{2,1,0:T(8,128)(2,1)}), bf16[16,16,640]{2,1,0:T(8,128)(2,1)S(1)}, u32[]{:S(2)}, u32[]{:S(2)}) async-start(bf16[16,16,640]{2,1,0:T(8,128)(2,1)} %shard_map.178), calls=%async_computation.1 | async-start | bytes 655360 | tf_op jit(solution)/shard_map/all_to_all | solution.py:349
  64.0 3.4 %copy-start.6 = (bf16[320,2560]{1,0:T(8,128)(2,1)S(1)}, bf16[320,2560]{1,0:T(8,128)(2,1)}, u32[]{:S(2)}) copy-start(bf16[320,2560]{1,0:T(8,128)(2,1)} %geglu_ref.1) | copy-start | bytes 4915204
  64.0 3.4 %copy-start.7 = (bf16[1280,320]{0,1:T(8,128)(2,1)S(1)}, bf16[1280,320]{0,1:T(8,128)(2,1)}, u32[]{:S(2)}) copy-start(bf16[1280,320]{0,1:T(8,128)(2,1)} %param.33) | copy-start | bytes 2457604

commit v4 on v3

--- a/solution.py
+++ b/solution.py
@@ -20,7 +20,6 @@
 COLS = 128
 PATCHES = 32
 TOKENS_FLOPS = 5*10**9
-FAN_FLOPS = 10**6
 MIB = 1024 * 1024
 
 
@@ -36,13 +35,6 @@
     )
     last = jnp.concatenate([rows[16:, q * PIECE : (q + 1) * PIECE] for q in range(4)], axis=0)
     out_ref[...] = jnp.concatenate([rows[:16], last], axis=1).astype(jnp.bfloat16)
-
-
-def fan_kernel(own_ref, other_ref, place_ref, out_ref):
-    y = place_ref[1]
-    for x in range(4):
-        out_ref[x, y] = own_ref[...]
-        out_ref[x, 1 - y] = other_ref[...]
 
 
 def tokens_kernel(*refs):
@@ -320,9 +312,9 @@
     mirrored = [(h * 4 + l, (1 - h) * 4 + 3 - l) for h in range(2) for l in range(4)]
     other = lax.ppermute(packed, ("yh", "yl"), mirrored)
     place = jnp.stack([lax.axis_index(a) for a in frame]).astype(jnp.int32)
-    fanned = call(
-        fan_kernel, (4, 2, 16, 3 * TAPS_PAD + PIECE), FAN_FLOPS, in_specs=[None, None, pltpu.SMEM]
-    )(packed, other, place)
+    upper_half = place[1] == 0
+    pair = jnp.stack([jnp.where(upper_half, packed, other), jnp.where(upper_half, other, packed)])
+    fanned = jnp.broadcast_to(pair[None], (4,) + pair.shape)
     weight = lax.all_to_all(fanned, "x", 0, 0, tiled=True).reshape(8, 16, 3 * TAPS_PAD + PIECE)
 
     rims = stale_edges.transpose(0, 1, 3, 2)

time: 88.2 us -> 87.8 us (level)
  Pallas kernels: 13.9 us -> 12.3 us
  local copies, waits for them, and re-layouts: 2.22 us -> 3.26 us
    pallas_call x1 -> x0, Pallas kernels: 1.59 us -> none  [per_device(): call(fan_kernel, (4, 2, 16, 3 * TAPS_PAD + PIECE), FAN_FLOPS, in_specs=[N...]
    broadcast_in_dim x0 -> x1, local copies, waits for them, and re-layouts: none -> 1.04 us  [per_device(): fanned = jnp.broadcast_to(pair[None], (4,) + pair.shape)]
  transfers between devices with their start and end apart: 6 -> 6, of which waited for: 3 -> 3; matrix products, arithmetic and copies ran while one was open for 1% -> 3% of each run, Pallas kernels for 5% -> 3%
where the time goes in v4:
time: 87.8 us; the launch traced here: 87.3 us
  starting transfers between devices  37.9 us (43%)
  blocking collectives  16.7 us (19%)
  waiting for transfers between devices  16.5 us (19%)
  Pallas kernels  12.3 us (14%)
  local copies, waits for them, and re-layouts  3.26 us (4%)
    all_to_all x1, blocking collectives, per_device(): returned = lax.all_to_all(done, frame, 0, 0, tiled=True)  16.7 us
    all_to_all x1, waiting for transfers between devices, per_device(): owned = lax.all_to_all(outgoing, frame, 0, 0, tiled=True)  14.5 us
    ppermute x1, starting transfers between devices, per_device(): lax.ppermute(rims[:, 0], patch, [(i + 1, i) for i in range(PATCHES - 1)])  10.3 us
    all_to_all x1, starting transfers between devices, per_device(): owned = lax.all_to_all(outgoing, frame, 0, 0, tiled=True)  9.51 us
    ppermute x1, starting transfers between devices, per_device(): other = lax.ppermute(packed, ('yh', 'yl'), mirrored)  5.77 us
    ppermute x1, starting transfers between devices, per_device(): theirs = lax.ppermute(weight, 'c', [(0, 1), (1, 0)])  4.34 us
    all_to_all x1, starting transfers between devices, per_device(): lax.all_to_all(fanned, 'x', 0, 0, tiled=True)  4.01 us
    ppermute x1, starting transfers between devices, per_device(): lax.ppermute(rims[:, 1], patch, [(i, i + 1) for i in range(PATCHES - 1)])  4 us
  transfers between devices with their start and end apart: 6, of which 3 were waited for; matrix products, arithmetic and copies ran while one was open for 3% of the time, Pallas kernels for 3%

profile of v4, /device:TPU:9, one launch (start us, length us, event | category | flops | bytes accessed | tf_op | source)
XLA Modules:
  0.0 87.3 jit_solution(6536146008949664038)
XLA Ops:
  0.0 0.9 %copy-done.4 = bf16[3,3,320,20]{2,3,1,0:T(8,128)(2,1)S(1)} copy-done((bf16[3,3,320,20]{2,3,1,0:T(8,128)(2,1)S(1)}, bf16[3,3,320,20]{2,3,1,0:T(8,128)(2,1)}, u32[]{:S(2)}) %copy-start.4) | copy-done | bytes 115224
  0.9 0.1 shard_map.172
  1.0 5.8 %collective-permute-start = (bf16[16,3840]{1,0:T(8,128)(2,1)S(1)}, bf16[16,3840]{1,0:T(8,128)(2,1)S(1)}, u32[]{:S(2)}, u32[]{:S(2)}) collective-permute-start(bf16[16,3840]{1,0:T(8,128)(2,1)S(1)} %shard_map.172), channel_id=1, source_target_pairs={{0,88},{8,80},{16,72},{24,64},{64,24},{72,16},{80,8},{88,0},{1,89}... | collective-permute-start | bytes 368648 | tf_op jit(solution)/shard_map/ppermute | solution.py:313
  6.8 1.1 %copy.22 = bf16[4,2,128,320]{2,3,0,1:T(8,128)(2,1)S(1)} copy(bf16[4,2,128,320]{2,3,1,0:T(8,128)(2,1)} %param.19) | data formatting | bytes 1310720 | tf_op args[1]
  8.0 4.0 %collective-permute-start.1 = (bf16[4,320,128]{2,1,0:T(8,128)(2,1)S(1)}, bf16[4,320,128]{2,1,0:T(8,128)(2,1)S(1)}, u32[]{:S(2)}, u32[]{:S(2)}) collective-permute-start(bf16[4,320,128]{2,1,0:T(8,128)(2,1)S(1)} %get-tuple-element.22), channel_id=1, source_target_pairs={{0,1},{1,2},{2,3},{3,4},{4,5},{5,6},{6,7},{7,8},{8,9},{9,10},{10,1... | collective-permute-start | bytes 983048 | tf_op jit(solution)/shard_map/ppermute | solution.py:321
  12.1 1.0 %broadcast_in_dim.33 = bf16[4,2,16,3840]{3,2,1,0:T(8,128)(2,1)} broadcast(bf16[2,16,3840]{2,1,0:T(8,128)(2,1)S(1)} %pad_maximum_fusion), dimensions={1,2,3} | broadcast | bytes 1228800 | tf_op jit(solution)/shard_map/broadcast_in_dim | solution.py:317
  13.1 4.0 %all-to-all-start = ((bf16[4,2,16,3840]{3,2,1,0:T(8,128)(2,1)}), bf16[4,2,16,3840]{3,2,1,0:T(8,128)(2,1)S(1)}, u32[]{:S(2)}, u32[]{:S(2)}) async-start(bf16[4,2,16,3840]{3,2,1,0:T(8,128)(2,1)} %broadcast_in_dim.33), calls=%async_computation | async-start | bytes 1966080 | tf_op jit(solution)/shard_map/all_to_all | solution.py:318
  17.1 10.3 %collective-permute-start.2 = (bf16[4,320,128]{2,1,0:T(8,128)(2,1)S(1)}, bf16[4,320,128]{2,1,0:T(8,128)(2,1)S(1)}, u32[]{:S(2)}, u32[]{:S(2)}) collective-permute-start(bf16[4,320,128]{2,1,0:T(8,128)(2,1)S(1)} %get-tuple-element.21), channel_id=1, source_target_pairs={{1,0},{2,1},{3,2},{4,3},{5,4},{6,5},{7,6},{8,7},{9,8},{10,9},{11,1... | collective-permute-start | bytes 983048 | tf_op jit(solution)/shard_map/ppermute | solution.py:322
  27.5 0.1 pad_add_fusion.place_ref
  27.6 0.7 shard_map.175
  28.3 0.2 shard_map.173.upper_ref
  28.5 1.5 %all-to-all-done = bf16[4,2,16,3840]{3,2,1,0:T(8,128)(2,1)S(1)} async-done(((bf16[4,2,16,3840]{3,2,1,0:T(8,128)(2,1)}), bf16[4,2,16,3840]{3,2,1,0:T(8,128)(2,1)S(1)}, u32[]{:S(2)}, u32[]{:S(2)}) %all-to-all-start) | async-done | bytes 983072 | tf_op jit(solution)/shard_map/all_to_all | solution.py:318
  30.1 4.3 %collective-permute-start.3 = (bf16[8,16,3840]{2,1,0:T(8,128)(2,1)S(1)}, bf16[8,16,3840]{2,1,0:T(8,128)(2,1)S(1)}, u32[]{:S(2)}, u32[]{:S(2)}) collective-permute-start(bf16[8,16,3840]{2,1,0:T(8,128)(2,1)S(1)} %bitcast.25), channel_id=1, source_target_pairs={{0,32},{32,0},{1,33},{33,1},{2,34},{34,2},{3,35},{35,3},{4,36},{36... | collective-permute-start | bytes 2949128 | tf_op jit(solution)/shard_map/ppermute | solution.py:334
  34.4 0.2 shard_map.174.below_ref
  34.6 1.4 %shard_map.176.first_ref = f32[512,320]{1,0:T(8,128)S(1)} custom-call(bf16[512,640]{1,0:T(8,128)(2,1)S(1)} %shard_map.173.upper_ref, bf16[512,384]{1,0:T(8,128)(2,1)S(1)} %shard_map.174.below_ref, bf16[8,16,3840]{2,1,0:T(8,128)(2,1)S(1)} %bitcast.26, f32[8,320]{1,0:T(8,128)S(1)} %get-tuple-element.15.bias_ref, bf16[320,320]{1,0:T(8,128)(2,1)S(1)} %get-tuple-element.16.order_ref), custom_call_target="tpu_custom_call" | custom-call | flops 1000000000 | bytes 4194304 | tf_op jit(solution)/shard_map/pallas_call | solution.py:335
  36.1 0.5 collective-permute-done.3.w_ref
  36.6 2.2 %shard_map.177 = bf16[16,16,640]{2,1,0:T(8,128)(2,1)} custom-call(bf16[512,640]{1,0:T(8,128)(2,1)S(1)} %shard_map.173.upper_ref, bf16[512,384]{1,0:T(8,128)(2,1)S(1)} %shard_map.174.below_ref, bf16[8,16,3840]{2,1,0:T(8,128)(2,1)S(1)} %collective-permute-done.3.w_ref, f32[8,320]{1,0:T(8,128)S(1)} %get-tuple-element.15.bias_ref, ...), custom_call_target="tpu_custom_call" | custom-call | flops 1000000000 | bytes 4194304 | tf_op jit(solution)/shard_map/pallas_call | solution.py:338
  38.8 9.5 %all-to-all-start.1 = ((bf16[16,16,640]{2,1,0:T(8,128)(2,1)}), bf16[16,16,640]{2,1,0:T(8,128)(2,1)S(1)}, u32[]{:S(2)}, u32[]{:S(2)}) async-start(bf16[16,16,640]{2,1,0:T(8,128)(2,1)} %shard_map.177), calls=%async_computation.1 | async-start | bytes 655360 | tf_op jit(solution)/shard_map/all_to_all | solution.py:341
  48.5 0.5 shard_map.178
  49.0 14.5 %all-to-all-done.1.x_ref = bf16[16,16,640]{2,1,0:T(8,128)(2,1)S(1)} async-done(((bf16[16,16,640]{2,1,0:T(8,128)(2,1)}), bf16[16,16,640]{2,1,0:T(8,128)(2,1)S(1)}, u32[]{:S(2)}, u32[]{:S(2)}) %all-to-all-start.1) | async-done | bytes 327712 | tf_op jit(solution)/shard_map/all_to_all | solution.py:341
  63.5 3.4 %shard_map.179.middle_ref = bf16[512,320]{1,0:T(8,128)(2,1)S(1)} custom-call(bf16[16,16,640]{2,1,0:T(8,128)(2,1)S(1)} %all-to-all-done.1.x_ref, bf16[320,1024]{1,0:T(8,128)(2,1)S(1)} %get-tuple-element.18.spread_ref, bf16[640,320]{1,0:T(8,128)(2,1)S(1)} %get-tuple-element.19.square_ref, f32[72,320]{1,0:T(8,128)S(1)} %get-tuple-element.20.vectors_ref), custom_call_target="tpu_custom_call" | custom-call | flops 1000000000 | bytes 4194304 | tf_op jit(solution)/shard_map/pallas_call | solution.py:361
  67.0 2.6 %shard_map.180 = bf16[16,16,640]{2,1,0:T(8,128)(2,1)S(1)} custom-call(bf16[512,320]{1,0:T(8,128)(2,1)S(1)} %shard_map.179.middle_ref, f32[72,320]{1,0:T(8,128)S(1)} %get-tuple-element.20.vectors_ref, bf16[320,2560]{1,0:T(8,128)(2,1)S(1)} %copy-done.6, f32[1,2560]{1,0:T(1,128)S(1)} %broadcast_in_dim.41.geglu_bias_ref, bf16[320,1280]{1,0:T(8,128)(2,1)S(1)} %bitcast.28), custom_call_target="tpu_custom_call" | custom-call | flops 1000000000 | bytes 4194304 | tf_op jit(solution)/shard_map/pallas_call | solution.py:368
  69.6 16.7 %all_to_all.15.x_ref = bf16[16,16,640]{2,1,0:T(8,128)(2,1)S(1)} all-to-all(bf16[16,16,640]{2,1,0:T(8,128)(2,1)S(1)} %shard_map.180), channel_id=1, replica_groups=mesh['x'=4,'yh'=2,'c'=2,'yl'=4,'z'=8] {'x','yh','c'}, dimensions={0} | all-to-all | bytes 655360 | tf_op jit(solution)/shard_map/all_to_all | solution.py:371
  86.3 1.0 %shard_map.181 = bf16[4,320,128]{2,1,0:T(8,128)(2,1)} custom-call(bf16[16,16,640]{2,1,0:T(8,128)(2,1)S(1)} %all_to_all.15.x_ref), custom_call_target="tpu_custom_call" | custom-call | flops 1000000 | bytes 4194304 | tf_op jit(solution)/shard_map/pallas_call | solution.py:372
  (47 shorter events, 0.2 us)
Async XLA Ops:
  0.0 0.9 %copy-start.4 = (bf16[3,3,320,20]{2,3,1,0:T(8,128)(2,1)S(1)}, bf16[3,3,320,20]{2,3,1,0:T(8,128)(2,1)}, u32[]{:S(2)}) copy-start(bf16[3,3,320,20]{2,3,1,0:T(8,128)(2,1)} %param.20) | copy-start | bytes 345604
  1.0 11.0 %collective-permute-start = (bf16[16,3840]{1,0:T(8,128)(2,1)S(1)}, bf16[16,3840]{1,0:T(8,128)(2,1)S(1)}, u32[]{:S(2)}, u32[]{:S(2)}) collective-permute-start(bf16[16,3840]{1,0:T(8,128)(2,1)S(1)} %shard_map.172), channel_id=1, source_target_pairs={{0,88},{8,80},{16,72},{24,64},{64,24},{72,16},{80,8},{88,0},{1,89}... | collective-permute-start | bytes 368648 | tf_op jit(solution)/shard_map/ppermute | solution.py:313
  8.0 20.3 %collective-permute-start.1 = (bf16[4,320,128]{2,1,0:T(8,128)(2,1)S(1)}, bf16[4,320,128]{2,1,0:T(8,128)(2,1)S(1)}, u32[]{:S(2)}, u32[]{:S(2)}) collective-permute-start(bf16[4,320,128]{2,1,0:T(8,128)(2,1)S(1)} %get-tuple-element.22), channel_id=1, source_target_pairs={{0,1},{1,2},{2,3},{3,4},{4,5},{5,6},{6,7},{7,8},{8,9},{9,10},{10,1... | collective-permute-start | bytes 983048 | tf_op jit(solution)/shard_map/ppermute | solution.py:321
  12.1 15.4 %copy-start.10 = (f32[320]{0:T(512)S(1)}, f32[320]{0:T(512)}, u32[]{:S(2)}) copy-start(f32[320]{0:T(512)} %param.21) | copy-start | bytes 3844
  12.1 16.2 %copy-start.8 = (bf16[4,1,128,320]{2,3,1,0:T(8,128)(2,1)S(1)}, bf16[4,1,128,320]{2,3,1,0:T(8,128)(2,1)}, u32[]{:S(2)}) copy-start(bf16[4,1,128,320]{2,3,1,0:T(8,128)(2,1)} %param.18) | copy-start | bytes 983044
  13.1 16.9 %all-to-all-start = ((bf16[4,2,16,3840]{3,2,1,0:T(8,128)(2,1)}), bf16[4,2,16,3840]{3,2,1,0:T(8,128)(2,1)S(1)}, u32[]{:S(2)}, u32[]{:S(2)}) async-start(bf16[4,2,16,3840]{3,2,1,0:T(8,128)(2,1)} %broadcast_in_dim.33), calls=%async_computation | async-start | bytes 1966080 | tf_op jit(solution)/shard_map/all_to_all | solution.py:318
  17.1 17.3 %collective-permute-start.2 = (bf16[4,320,128]{2,1,0:T(8,128)(2,1)S(1)}, bf16[4,320,128]{2,1,0:T(8,128)(2,1)S(1)}, u32[]{:S(2)}, u32[]{:S(2)}) collective-permute-start(bf16[4,320,128]{2,1,0:T(8,128)(2,1)S(1)} %get-tuple-element.21), channel_id=1, source_target_pairs={{1,0},{2,1},{3,2},{4,3},{5,4},{6,5},{7,6},{8,7},{9,8},{10,9},{11,1... | collective-permute-start | bytes 983048 | tf_op jit(solution)/shard_map/ppermute | solution.py:322
  30.1 6.5 %collective-permute-start.3 = (bf16[8,16,3840]{2,1,0:T(8,128)(2,1)S(1)}, bf16[8,16,3840]{2,1,0:T(8,128)(2,1)S(1)}, u32[]{:S(2)}, u32[]{:S(2)}) collective-permute-start(bf16[8,16,3840]{2,1,0:T(8,128)(2,1)S(1)} %bitcast.25), channel_id=1, source_target_pairs={{0,32},{32,0},{1,33},{33,1},{2,34},{34,2},{3,35},{35,3},{4,36},{36... | collective-permute-start | bytes 2949128 | tf_op jit(solution)/shard_map/ppermute | solution.py:334
  36.0 12.3 %copy-start.11 = (f32[320]{0:T(512)S(1)}, f32[320]{0:T(512)}, u32[]{:S(2)}) copy-start(f32[320]{0:T(512)} %param.22) | copy-start | bytes 3844
  36.0 12.3 %copy-start.12 = (f32[320]{0:T(512)S(1)}, f32[320]{0:T(512)}, u32[]{:S(2)}) copy-start(f32[320]{0:T(512)} %param.23) | copy-start | bytes 3844
  36.0 12.3 %copy-start.13 = (f32[320]{0:T(512)S(1)}, f32[320]{0:T(512)}, u32[]{:S(2)}) copy-start(f32[320]{0:T(512)} %param.28) | copy-start | bytes 3844
  36.0 12.3 %copy-start.14 = (f32[320]{0:T(512)S(1)}, f32[320]{0:T(512)}, u32[]{:S(2)}) copy-start(f32[320]{0:T(512)} %param.29) | copy-start | bytes 3844
  36.0 12.3 %copy-start.15 = (f32[320]{0:T(512)S(1)}, f32[320]{0:T(512)}, u32[]{:S(2)}) copy-start(f32[320]{0:T(512)} %param.30) | copy-start | bytes 3844
  36.0 12.3 %copy-start.16 = (f32[320]{0:T(512)S(1)}, f32[320]{0:T(512)}, u32[]{:S(2)}) copy-start(f32[320]{0:T(512)} %param.34) | copy-start | bytes 3844
  36.0 12.4 %copy-start.9 = (f32[2560]{0:T(1024)S(1)}, f32[2560]{0:T(1024)}, u32[]{:S(2)}) copy-start(f32[2560]{0:T(1024)} %param.32) | copy-start | bytes 30724
  36.1 12.4 %copy-start = (bf16[320,320]{1,0:T(8,128)(2,1)S(1)}, bf16[320,320]{1,0:T(8,128)(2,1)}, u32[]{:S(2)}) copy-start(bf16[320,320]{1,0:T(8,128)(2,1)} %refs_0_) | copy-start | bytes 614404
  36.1 12.4 %copy-start.1 = (bf16[320,320]{1,0:T(8,128)(2,1)S(1)}, bf16[320,320]{1,0:T(8,128)(2,1)}, u32[]{:S(2)}) copy-start(bf16[320,320]{1,0:T(8,128)(2,1)} %refs_1_.1) | copy-start | bytes 614404
  36.1 12.4 %copy-start.2 = (bf16[320,320]{1,0:T(8,128)(2,1)S(1)}, bf16[320,320]{1,0:T(8,128)(2,1)}, u32[]{:S(2)}) copy-start(bf16[320,320]{1,0:T(8,128)(2,1)} %refs_2_.1) | copy-start | bytes 614404
  36.1 12.4 %copy-start.3 = (bf16[320,320]{1,0:T(8,128)(2,1)S(1)}, bf16[320,320]{1,0:T(8,128)(2,1)}, u32[]{:S(2)}) copy-start(bf16[320,320]{1,0:T(8,128)(2,1)} %refs_3_.1) | copy-start | bytes 614404
  36.1 12.4 %copy-start.5 = (f32[64,320]{1,0:T(8,128)S(1)}, f32[64,320]{1,0:T(8,128)}, u32[]{:S(2)}) copy-start(f32[64,320]{1,0:T(8,128)} %constant.20.clone.refs_4_) | copy-start | bytes 245764
  38.8 24.8 %all-to-all-start.1 = ((bf16[16,16,640]{2,1,0:T(8,128)(2,1)}), bf16[16,16,640]{2,1,0:T(8,128)(2,1)S(1)}, u32[]{:S(2)}, u32[]{:S(2)}) async-start(bf16[16,16,640]{2,1,0:T(8,128)(2,1)} %shard_map.177), calls=%async_computation.1 | async-start | bytes 655360 | tf_op jit(solution)/shard_map/all_to_all | solution.py:341
  63.5 3.4 %copy-start.6 = (bf16[320,2560]{1,0:T(8,128)(2,1)S(1)}, bf16[320,2560]{1,0:T(8,128)(2,1)}, u32[]{:S(2)}) copy-start(bf16[320,2560]{1,0:T(8,128)(2,1)} %geglu_ref.1) | copy-start | bytes 4915204
  63.5 3.4 %copy-start.7 = (bf16[1280,320]{0,1:T(8,128)(2,1)S(1)}, bf16[1280,320]{0,1:T(8,128)(2,1)}, u32[]{:S(2)}) copy-start(bf16[1280,320]{0,1:T(8,128)(2,1)} %param.33) | copy-start | bytes 2457604

commit v5 on v4

--- a/solution.py
+++ b/solution.py
@@ -223,6 +223,7 @@
     normed_two = norm_rows(middle, second_gain, second_shift).astype(jnp.bfloat16)
     total = middle + down_bias
     step = 256
+    pieces = []
     for start in range(0, FF, step):
         lanes = slice(start, start + step)
         gates = slice(FF + start, FF + start + step)
@@ -235,12 +236,13 @@
             + geglu_bias_ref[:, gates]
         )
         hidden = value * (0.5 * gate * (1.0 + lax.erf(gate * (1.0 / math.sqrt(2.0)))))
-        total = total + lax.dot_general(
-            hidden.astype(jnp.bfloat16),
-            down_ref[:, lanes],
-            (((1,), (1,)), ((), ())),
-            preferred_element_type=jnp.float32,
-        )
+        pieces.append(hidden.astype(jnp.bfloat16))
+    total = total + lax.dot_general(
+        jnp.concatenate(pieces, axis=1),
+        down_ref[...],
+        (((1,), (1,)), ((), ())),
+        preferred_element_type=jnp.float32,
+    )
     for p in range(pixels):
         near = total[p * FRAMES : p * FRAMES + 32]
         far = total[p * FRAMES + 32 : (p + 1) * FRAMES]

time: 87.8 us -> 87.7 us (level)
  no operation moved by 1% of the time
where the time goes in v5:
time: 87.7 us; the launch traced here: 87.3 us
  starting transfers between devices  37.9 us (43%)
  blocking collectives  16.7 us (19%)
  waiting for transfers between devices  16.5 us (19%)
  Pallas kernels  12.3 us (14%)
  local copies, waits for them, and re-layouts  3.26 us (4%)
    all_to_all x1, blocking collectives, per_device(): returned = lax.all_to_all(done, frame, 0, 0, tiled=True)  16.7 us
    all_to_all x1, waiting for transfers between devices, per_device(): owned = lax.all_to_all(outgoing, frame, 0, 0, tiled=True)  14.5 us
    ppermute x1, starting transfers between devices, per_device(): lax.ppermute(rims[:, 0], patch, [(i + 1, i) for i in range(PATCHES - 1)])  10.3 us
    all_to_all x1, starting transfers between devices, per_device(): owned = lax.all_to_all(outgoing, frame, 0, 0, tiled=True)  9.51 us
    ppermute x1, starting transfers between devices, per_device(): other = lax.ppermute(packed, ('yh', 'yl'), mirrored)  5.77 us
    ppermute x1, starting transfers between devices, per_device(): theirs = lax.ppermute(weight, 'c', [(0, 1), (1, 0)])  4.34 us
    all_to_all x1, starting transfers between devices, per_device(): lax.all_to_all(fanned, 'x', 0, 0, tiled=True)  4.01 us
    ppermute x1, starting transfers between devices, per_device(): lax.ppermute(rims[:, 1], patch, [(i, i + 1) for i in range(PATCHES - 1)])  4 us
  transfers between devices with their start and end apart: 6, of which 3 were waited for; matrix products, arithmetic and copies ran while one was open for 3% of the time, Pallas kernels for 3%

profile of v5, /device:TPU:9, one launch (start us, length us, event | category | flops | bytes accessed | tf_op | source)
XLA Modules:
  0.0 87.3 jit_solution(8778133147628743331)
XLA Ops:
  0.0 0.9 %copy-done.4 = bf16[3,3,320,20]{2,3,1,0:T(8,128)(2,1)S(1)} copy-done((bf16[3,3,320,20]{2,3,1,0:T(8,128)(2,1)S(1)}, bf16[3,3,320,20]{2,3,1,0:T(8,128)(2,1)}, u32[]{:S(2)}) %copy-start.4) | copy-done | bytes 115224
  0.9 0.1 shard_map.172
  1.0 5.8 %collective-permute-start = (bf16[16,3840]{1,0:T(8,128)(2,1)S(1)}, bf16[16,3840]{1,0:T(8,128)(2,1)S(1)}, u32[]{:S(2)}, u32[]{:S(2)}) collective-permute-start(bf16[16,3840]{1,0:T(8,128)(2,1)S(1)} %shard_map.172), channel_id=1, source_target_pairs={{0,88},{8,80},{16,72},{24,64},{64,24},{72,16},{80,8},{88,0},{1,89}... | collective-permute-start | bytes 368648 | tf_op jit(solution)/shard_map/ppermute | solution.py:315
  6.8 1.1 %copy.22 = bf16[4,2,128,320]{2,3,0,1:T(8,128)(2,1)S(1)} copy(bf16[4,2,128,320]{2,3,1,0:T(8,128)(2,1)} %param.19) | data formatting | bytes 1310720 | tf_op args[1]
  8.0 4.0 %collective-permute-start.1 = (bf16[4,320,128]{2,1,0:T(8,128)(2,1)S(1)}, bf16[4,320,128]{2,1,0:T(8,128)(2,1)S(1)}, u32[]{:S(2)}, u32[]{:S(2)}) collective-permute-start(bf16[4,320,128]{2,1,0:T(8,128)(2,1)S(1)} %get-tuple-element.22), channel_id=1, source_target_pairs={{0,1},{1,2},{2,3},{3,4},{4,5},{5,6},{6,7},{7,8},{8,9},{9,10},{10,1... | collective-permute-start | bytes 983048 | tf_op jit(solution)/shard_map/ppermute | solution.py:323
  12.1 1.0 %broadcast_in_dim.33 = bf16[4,2,16,3840]{3,2,1,0:T(8,128)(2,1)} broadcast(bf16[2,16,3840]{2,1,0:T(8,128)(2,1)S(1)} %pad_maximum_fusion), dimensions={1,2,3} | broadcast | bytes 1228800 | tf_op jit(solution)/shard_map/broadcast_in_dim | solution.py:319
  13.1 4.0 %all-to-all-start = ((bf16[4,2,16,3840]{3,2,1,0:T(8,128)(2,1)}), bf16[4,2,16,3840]{3,2,1,0:T(8,128)(2,1)S(1)}, u32[]{:S(2)}, u32[]{:S(2)}) async-start(bf16[4,2,16,3840]{3,2,1,0:T(8,128)(2,1)} %broadcast_in_dim.33), calls=%async_computation | async-start | bytes 1966080 | tf_op jit(solution)/shard_map/all_to_all | solution.py:320
  17.1 10.3 %collective-permute-start.2 = (bf16[4,320,128]{2,1,0:T(8,128)(2,1)S(1)}, bf16[4,320,128]{2,1,0:T(8,128)(2,1)S(1)}, u32[]{:S(2)}, u32[]{:S(2)}) collective-permute-start(bf16[4,320,128]{2,1,0:T(8,128)(2,1)S(1)} %get-tuple-element.21), channel_id=1, source_target_pairs={{1,0},{2,1},{3,2},{4,3},{5,4},{6,5},{7,6},{8,7},{9,8},{10,9},{11,1... | collective-permute-start | bytes 983048 | tf_op jit(solution)/shard_map/ppermute | solution.py:324
  27.5 0.1 pad_add_fusion.place_ref
  27.6 0.7 shard_map.175
  28.3 0.2 shard_map.173.upper_ref
  28.5 1.5 %all-to-all-done = bf16[4,2,16,3840]{3,2,1,0:T(8,128)(2,1)S(1)} async-done(((bf16[4,2,16,3840]{3,2,1,0:T(8,128)(2,1)}), bf16[4,2,16,3840]{3,2,1,0:T(8,128)(2,1)S(1)}, u32[]{:S(2)}, u32[]{:S(2)}) %all-to-all-start) | async-done | bytes 983072 | tf_op jit(solution)/shard_map/all_to_all | solution.py:320
  30.1 4.3 %collective-permute-start.3 = (bf16[8,16,3840]{2,1,0:T(8,128)(2,1)S(1)}, bf16[8,16,3840]{2,1,0:T(8,128)(2,1)S(1)}, u32[]{:S(2)}, u32[]{:S(2)}) collective-permute-start(bf16[8,16,3840]{2,1,0:T(8,128)(2,1)S(1)} %bitcast.25), channel_id=1, source_target_pairs={{0,32},{32,0},{1,33},{33,1},{2,34},{34,2},{3,35},{35,3},{4,36},{36... | collective-permute-start | bytes 2949128 | tf_op jit(solution)/shard_map/ppermute | solution.py:336
  34.4 0.2 shard_map.174.below_ref
  34.6 1.4 %shard_map.176.first_ref = f32[512,320]{1,0:T(8,128)S(1)} custom-call(bf16[512,640]{1,0:T(8,128)(2,1)S(1)} %shard_map.173.upper_ref, bf16[512,384]{1,0:T(8,128)(2,1)S(1)} %shard_map.174.below_ref, bf16[8,16,3840]{2,1,0:T(8,128)(2,1)S(1)} %bitcast.26, f32[8,320]{1,0:T(8,128)S(1)} %get-tuple-element.15.bias_ref, bf16[320,320]{1,0:T(8,128)(2,1)S(1)} %get-tuple-element.16.order_ref), custom_call_target="tpu_custom_call" | custom-call | flops 1000000000 | bytes 4194304 | tf_op jit(solution)/shard_map/pallas_call | solution.py:337
  36.1 0.5 collective-permute-done.3.w_ref
  36.6 2.2 %shard_map.177 = bf16[16,16,640]{2,1,0:T(8,128)(2,1)} custom-call(bf16[512,640]{1,0:T(8,128)(2,1)S(1)} %shard_map.173.upper_ref, bf16[512,384]{1,0:T(8,128)(2,1)S(1)} %shard_map.174.below_ref, bf16[8,16,3840]{2,1,0:T(8,128)(2,1)S(1)} %collective-permute-done.3.w_ref, f32[8,320]{1,0:T(8,128)S(1)} %get-tuple-element.15.bias_ref, ...), custom_call_target="tpu_custom_call" | custom-call | flops 1000000000 | bytes 4194304 | tf_op jit(solution)/shard_map/pallas_call | solution.py:340
  38.8 9.5 %all-to-all-start.1 = ((bf16[16,16,640]{2,1,0:T(8,128)(2,1)}), bf16[16,16,640]{2,1,0:T(8,128)(2,1)S(1)}, u32[]{:S(2)}, u32[]{:S(2)}) async-start(bf16[16,16,640]{2,1,0:T(8,128)(2,1)} %shard_map.177), calls=%async_computation.1 | async-start | bytes 655360 | tf_op jit(solution)/shard_map/all_to_all | solution.py:343
  48.5 0.5 shard_map.178
  49.0 14.5 %all-to-all-done.1.x_ref = bf16[16,16,640]{2,1,0:T(8,128)(2,1)S(1)} async-done(((bf16[16,16,640]{2,1,0:T(8,128)(2,1)}), bf16[16,16,640]{2,1,0:T(8,128)(2,1)S(1)}, u32[]{:S(2)}, u32[]{:S(2)}) %all-to-all-start.1) | async-done | bytes 327712 | tf_op jit(solution)/shard_map/all_to_all | solution.py:343
  63.5 3.4 %shard_map.179.middle_ref = bf16[512,320]{1,0:T(8,128)(2,1)S(1)} custom-call(bf16[16,16,640]{2,1,0:T(8,128)(2,1)S(1)} %all-to-all-done.1.x_ref, bf16[320,1024]{1,0:T(8,128)(2,1)S(1)} %get-tuple-element.18.spread_ref, bf16[640,320]{1,0:T(8,128)(2,1)S(1)} %get-tuple-element.19.square_ref, f32[72,320]{1,0:T(8,128)S(1)} %get-tuple-element.20.vectors_ref), custom_call_target="tpu_custom_call" | custom-call | flops 1000000000 | bytes 4194304 | tf_op jit(solution)/shard_map/pallas_call | solution.py:363
  67.0 2.6 %shard_map.180 = bf16[16,16,640]{2,1,0:T(8,128)(2,1)S(1)} custom-call(bf16[512,320]{1,0:T(8,128)(2,1)S(1)} %shard_map.179.middle_ref, f32[72,320]{1,0:T(8,128)S(1)} %get-tuple-element.20.vectors_ref, bf16[320,2560]{1,0:T(8,128)(2,1)S(1)} %copy-done.6, f32[1,2560]{1,0:T(1,128)S(1)} %broadcast_in_dim.41.geglu_bias_ref, bf16[320,1280]{1,0:T(8,128)(2,1)S(1)} %bitcast.28), custom_call_target="tpu_custom_call" | custom-call | flops 1000000000 | bytes 4194304 | tf_op jit(solution)/shard_map/pallas_call | solution.py:370
  69.6 16.7 %all_to_all.15.x_ref = bf16[16,16,640]{2,1,0:T(8,128)(2,1)S(1)} all-to-all(bf16[16,16,640]{2,1,0:T(8,128)(2,1)S(1)} %shard_map.180), channel_id=1, replica_groups=mesh['x'=4,'yh'=2,'c'=2,'yl'=4,'z'=8] {'x','yh','c'}, dimensions={0} | all-to-all | bytes 655360 | tf_op jit(solution)/shard_map/all_to_all | solution.py:373
  86.3 1.0 %shard_map.181 = bf16[4,320,128]{2,1,0:T(8,128)(2,1)} custom-call(bf16[16,16,640]{2,1,0:T(8,128)(2,1)S(1)} %all_to_all.15.x_ref), custom_call_target="tpu_custom_call" | custom-call | flops 1000000 | bytes 4194304 | tf_op jit(solution)/shard_map/pallas_call | solution.py:374
  (47 shorter events, 0.2 us)
Async XLA Ops:
  0.0 0.9 %copy-start.4 = (bf16[3,3,320,20]{2,3,1,0:T(8,128)(2,1)S(1)}, bf16[3,3,320,20]{2,3,1,0:T(8,128)(2,1)}, u32[]{:S(2)}) copy-start(bf16[3,3,320,20]{2,3,1,0:T(8,128)(2,1)} %param.20) | copy-start | bytes 345604
  1.0 11.0 %collective-permute-start = (bf16[16,3840]{1,0:T(8,128)(2,1)S(1)}, bf16[16,3840]{1,0:T(8,128)(2,1)S(1)}, u32[]{:S(2)}, u32[]{:S(2)}) collective-permute-start(bf16[16,3840]{1,0:T(8,128)(2,1)S(1)} %shard_map.172), channel_id=1, source_target_pairs={{0,88},{8,80},{16,72},{24,64},{64,24},{72,16},{80,8},{88,0},{1,89}... | collective-permute-start | bytes 368648 | tf_op jit(solution)/shard_map/ppermute | solution.py:315
  8.0 20.3 %collective-permute-start.1 = (bf16[4,320,128]{2,1,0:T(8,128)(2,1)S(1)}, bf16[4,320,128]{2,1,0:T(8,128)(2,1)S(1)}, u32[]{:S(2)}, u32[]{:S(2)}) collective-permute-start(bf16[4,320,128]{2,1,0:T(8,128)(2,1)S(1)} %get-tuple-element.22), channel_id=1, source_target_pairs={{0,1},{1,2},{2,3},{3,4},{4,5},{5,6},{6,7},{7,8},{8,9},{9,10},{10,1... | collective-permute-start | bytes 983048 | tf_op jit(solution)/shard_map/ppermute | solution.py:323
  12.1 15.4 %copy-start.10 = (f32[320]{0:T(512)S(1)}, f32[320]{0:T(512)}, u32[]{:S(2)}) copy-start(f32[320]{0:T(512)} %param.21) | copy-start | bytes 3844
  12.1 16.2 %copy-start.8 = (bf16[4,1,128,320]{2,3,1,0:T(8,128)(2,1)S(1)}, bf16[4,1,128,320]{2,3,1,0:T(8,128)(2,1)}, u32[]{:S(2)}) copy-start(bf16[4,1,128,320]{2,3,1,0:T(8,128)(2,1)} %param.18) | copy-start | bytes 983044
  13.1 16.9 %all-to-all-start = ((bf16[4,2,16,3840]{3,2,1,0:T(8,128)(2,1)}), bf16[4,2,16,3840]{3,2,1,0:T(8,128)(2,1)S(1)}, u32[]{:S(2)}, u32[]{:S(2)}) async-start(bf16[4,2,16,3840]{3,2,1,0:T(8,128)(2,1)} %broadcast_in_dim.33), calls=%async_computation | async-start | bytes 1966080 | tf_op jit(solution)/shard_map/all_to_all | solution.py:320
  17.1 17.3 %collective-permute-start.2 = (bf16[4,320,128]{2,1,0:T(8,128)(2,1)S(1)}, bf16[4,320,128]{2,1,0:T(8,128)(2,1)S(1)}, u32[]{:S(2)}, u32[]{:S(2)}) collective-permute-start(bf16[4,320,128]{2,1,0:T(8,128)(2,1)S(1)} %get-tuple-element.21), channel_id=1, source_target_pairs={{1,0},{2,1},{3,2},{4,3},{5,4},{6,5},{7,6},{8,7},{9,8},{10,9},{11,1... | collective-permute-start | bytes 983048 | tf_op jit(solution)/shard_map/ppermute | solution.py:324
  30.1 6.5 %collective-permute-start.3 = (bf16[8,16,3840]{2,1,0:T(8,128)(2,1)S(1)}, bf16[8,16,3840]{2,1,0:T(8,128)(2,1)S(1)}, u32[]{:S(2)}, u32[]{:S(2)}) collective-permute-start(bf16[8,16,3840]{2,1,0:T(8,128)(2,1)S(1)} %bitcast.25), channel_id=1, source_target_pairs={{0,32},{32,0},{1,33},{33,1},{2,34},{34,2},{3,35},{35,3},{4,36},{36... | collective-permute-start | bytes 2949128 | tf_op jit(solution)/shard_map/ppermute | solution.py:336
  36.0 12.3 %copy-start.11 = (f32[320]{0:T(512)S(1)}, f32[320]{0:T(512)}, u32[]{:S(2)}) copy-start(f32[320]{0:T(512)} %param.22) | copy-start | bytes 3844
  36.0 12.3 %copy-start.12 = (f32[320]{0:T(512)S(1)}, f32[320]{0:T(512)}, u32[]{:S(2)}) copy-start(f32[320]{0:T(512)} %param.23) | copy-start | bytes 3844
  36.0 12.3 %copy-start.13 = (f32[320]{0:T(512)S(1)}, f32[320]{0:T(512)}, u32[]{:S(2)}) copy-start(f32[320]{0:T(512)} %param.28) | copy-start | bytes 3844
  36.0 12.3 %copy-start.14 = (f32[320]{0:T(512)S(1)}, f32[320]{0:T(512)}, u32[]{:S(2)}) copy-start(f32[320]{0:T(512)} %param.29) | copy-start | bytes 3844
  36.0 12.3 %copy-start.15 = (f32[320]{0:T(512)S(1)}, f32[320]{0:T(512)}, u32[]{:S(2)}) copy-start(f32[320]{0:T(512)} %param.30) | copy-start | bytes 3844
  36.0 12.3 %copy-start.16 = (f32[320]{0:T(512)S(1)}, f32[320]{0:T(512)}, u32[]{:S(2)}) copy-start(f32[320]{0:T(512)} %param.34) | copy-start | bytes 3844
  36.0 12.4 %copy-start.9 = (f32[2560]{0:T(1024)S(1)}, f32[2560]{0:T(1024)}, u32[]{:S(2)}) copy-start(f32[2560]{0:T(1024)} %param.32) | copy-start | bytes 30724
  36.1 12.4 %copy-start = (bf16[320,320]{1,0:T(8,128)(2,1)S(1)}, bf16[320,320]{1,0:T(8,128)(2,1)}, u32[]{:S(2)}) copy-start(bf16[320,320]{1,0:T(8,128)(2,1)} %refs_0_) | copy-start | bytes 614404
  36.1 12.4 %copy-start.1 = (bf16[320,320]{1,0:T(8,128)(2,1)S(1)}, bf16[320,320]{1,0:T(8,128)(2,1)}, u32[]{:S(2)}) copy-start(bf16[320,320]{1,0:T(8,128)(2,1)} %refs_1_.1) | copy-start | bytes 614404
  36.1 12.4 %copy-start.2 = (bf16[320,320]{1,0:T(8,128)(2,1)S(1)}, bf16[320,320]{1,0:T(8,128)(2,1)}, u32[]{:S(2)}) copy-start(bf16[320,320]{1,0:T(8,128)(2,1)} %refs_2_.1) | copy-start | bytes 614404
  36.1 12.4 %copy-start.3 = (bf16[320,320]{1,0:T(8,128)(2,1)S(1)}, bf16[320,320]{1,0:T(8,128)(2,1)}, u32[]{:S(2)}) copy-start(bf16[320,320]{1,0:T(8,128)(2,1)} %refs_3_.1) | copy-start | bytes 614404
  36.1 12.4 %copy-start.5 = (f32[64,320]{1,0:T(8,128)S(1)}, f32[64,320]{1,0:T(8,128)}, u32[]{:S(2)}) copy-start(f32[64,320]{1,0:T(8,128)} %constant.20.clone.refs_4_) | copy-start | bytes 245764
  38.8 24.8 %all-to-all-start.1 = ((bf16[16,16,640]{2,1,0:T(8,128)(2,1)}), bf16[16,16,640]{2,1,0:T(8,128)(2,1)S(1)}, u32[]{:S(2)}, u32[]{:S(2)}) async-start(bf16[16,16,640]{2,1,0:T(8,128)(2,1)} %shard_map.177), calls=%async_computation.1 | async-start | bytes 655360 | tf_op jit(solution)/shard_map/all_to_all | solution.py:343
  63.5 3.4 %copy-start.6 = (bf16[320,2560]{1,0:T(8,128)(2,1)S(1)}, bf16[320,2560]{1,0:T(8,128)(2,1)}, u32[]{:S(2)}) copy-start(bf16[320,2560]{1,0:T(8,128)(2,1)} %geglu_ref.1) | copy-start | bytes 4915204
  63.5 3.4 %copy-start.7 = (bf16[1280,320]{0,1:T(8,128)(2,1)S(1)}, bf16[1280,320]{0,1:T(8,128)(2,1)}, u32[]{:S(2)}) copy-start(bf16[1280,320]{0,1:T(8,128)(2,1)} %param.33) | copy-start | bytes 2457604
